TPU v7x, 32 devices: a whole 2x2x4 slice. The times are simulated.
32 devices in a mesh: shard: 4 (over y, core), rep: 8 (over z, x).
Axes of the slice: x: 2, y: 2, z: 4, core: 2. Of those that a mesh axis runs over, the one named last changes fastest.
Arguments:
- layer_input: bfloat16 [256, 197, 768], P(('shard', 'rep')), may hold values from -6 to 6
- out_cotangent: bfloat16 [256, 197, 768], P(('shard', 'rep')), may hold values from -6 to 6
- attention_params: float32 [2363136], P('shard'), may hold values from -2 to 2.5
- attention_moments: float32 [2, 2363136], P(None, 'shard'), may hold values from -0.2 to 0.2, as said below
- feedforward_params: float32 [4723968], P('shard'), may hold values from -2 to 2.5
- feedforward_moments: float32 [2, 4723968], P(None, 'shard'), may hold values from -0.2 to 0.2, as said below
- step_count: int32 [1], replicated, may hold values from 1 to 20
Outputs:
- layer_output: bfloat16 [256, 197, 768], P(('shard', 'rep'))
- input_grad: bfloat16 [256, 197, 768], P(('shard', 'rep'))
- attention_grad: float32 [2363136], P('shard')
- feedforward_grad: float32 [4723968], P('shard')
- attention_change: float32 [2363136], P('shard')
- attention_moments_new: float32 [2, 2363136], P(None, 'shard')
- feedforward_change: float32 [4723968], P('shard')
- feedforward_moments_new: float32 [2, 4723968], P(None, 'shard')
Inputs may be any that keep to these rules, and one draw needn't show every extreme that they name: `attention_moments`: row 1, the second moments, is positive. `feedforward_moments`: row 1, the second moments, is positive.
All inputs are finite; a program needn't handle non-finite values.
Results may differ from a plain program's by a relative error of at most 0.017.
The roundings to bfloat16 on the way count: a program that leaves them out, or rounds other values in their place, can miss the bound.
Values may be sent and summed in bfloat16 or wider, within the bound.
No kernel may reach another device: no remote copies, remote signals or barrier semaphores. Data moves between devices by JAX's collectives and lax.ppermute only.
A program may use at most 384 MiB of HBM per device.

v0:
```python
import functools

import jax
import jax.numpy as jnp
from jax import lax
from jax.experimental import pallas as pl
from jax.experimental.pallas import tpu as pltpu
from jax.sharding import PartitionSpec as P

D = 768
HEADS = 12
FF = 3072
T = 208

F32 = jnp.float32
BF = jnp.bfloat16

ln_eps = 1e-06
beta_one = 0.9
beta_two = 0.999
adam_eps = 1e-08
rate_matrix = 0.01
rate_vector = 0.1
decay_matrix = 0.05
root_half = 0.7071067811865476
inv_root_tau = 0.3989422804014327

MB = 1 << 20
LANES = 128
MARGIN = 8

ATTN_START = (12, 5, -3, 2)
FEED_START = (12, 2, 15, 5)


def attn_parts(share):
    if share < 3:
        return [(0, 16, 256 * part, 6 * part, 18) for part in range(3)]
    return [(0, 48, 0, 0, 6)]


def feed_parts(share):
    if share < 2:
        return [(j, 24, 384 * h, 12 * h + 6 * j, 24) for j in range(2) for h in range(2)]
    return [(j, 48, 0, 4608 * j, 6) for j in range(2)]


def attn_grad_parts(share):
    if share < 3:
        return [
            (g, 8, 128 * part, 3 * u, 3, 18 * 128 * u + 6 * part + 3 * g, 18)
            for g in range(2)
            for part in range(3)
            for u in range(2)
        ]
    return [(g, 24, 0, 0, 6, 6 * 384 * g, 6) for g in range(2)]


def feed_grad_parts(share):
    return [(box, groups, row, 0, 6, flat, stride) for box, groups, row, flat, stride in feed_parts(share)]


ATTN_EXTRA = (
    [(0, 0, 12), (12, 4602, 14)],
    [(25, 0, 5), (30, 4613, 3)],
    [(33, 0, 15), (48, 4605, 11)],
    [(58, 0, 2), (60, 4610, 6)],
)
FEED_EXTRA = (
    [(0, 0, 12), (12, 9204, 23)],
    [(34, 0, 2), (36, 9218, 9)],
    [(45, 0, 15), (60, 9225, 2)],
    [(61, 0, 5), (66, 9221, 6)],
)
ATTN_PUT = (
    [(0, 0, 12)],
    [(25, 0, 5), (30, 4613, 3)],
    [(48, 4605, 12)],
    [(58, 0, 2), (60, 4610, 6)],
)
FEED_PUT = (
    [(0, 0, 12)],
    [(34, 0, 2), (36, 9218, 9)],
    [(45, 0, 15)],
    [(61, 0, 5), (66, 9221, 6)],
)
EXTRA = 72


class Block:
    def __init__(self, base, boxes, start, parts, grad_parts, extra, put, matrices):
        self.base = base
        self.boxes, self.start, self.parts, self.grad_parts = boxes, start, parts, grad_parts
        self.extra, self.put = extra, put
        self.matrices = matrices


ATTN = Block(
    0, 1, ATTN_START, attn_parts, attn_grad_parts, ATTN_EXTRA, ATTN_PUT, ((1536, 1771008), (1772544, 2362368))
)
FEED = Block(
    EXTRA, 2, FEED_START, feed_parts, feed_grad_parts, FEED_EXTRA, FEED_PUT, ((1536, 2360832), (2363904, 4723200))
)


def params(limit=56):
    return pltpu.CompilerParams(vmem_limit_bytes=limit * MB)


def dot(a, b):
    return lax.dot_general(a, b, (((1,), (0,)), ((), ())), preferred_element_type=F32)


def dot_nt(a, b):
    return lax.dot_general(a, b, (((1,), (1,)), ((), ())), preferred_element_type=F32)


def dot_tn(a, b):
    return lax.dot_general(a, b, (((0,), (0,)), ((), ())), preferred_element_type=F32)


def normed_of(values):
    center = values - jnp.mean(values, axis=-1, keepdims=True)
    spread = lax.rsqrt(jnp.mean(center * center, axis=-1, keepdims=True) + ln_eps)
    return center * spread, spread


def whole(array):
    rank = len(array.shape)
    return pl.BlockSpec(array.shape, lambda *i: (0,) * rank, pipeline_mode=pl.Buffered(1))


def rows_of(count, width):
    return pl.BlockSpec((count, width), lambda i: (i, 0))


SMEM = pl.BlockSpec(memory_space=pltpu.SMEM)


def sds(shape, dtype):
    return jax.ShapeDtypeStruct(shape, dtype)


CHUNK = 2368


def prep_kernel(block, steps, shard_ref, flat_ref, *refs):
    *box_refs, extra_ref, held = refs
    step = pl.program_id(0)
    held[pl.ds(pl.multiple_of(MARGIN + CHUNK * step, 8), CHUNK), :] = flat_ref[...].reshape(CHUNK, LANES)

    @pl.when(step == steps - 1)
    def _():
        low = lax.broadcasted_iota(jnp.int32, (8, LANES), 1) < 64
        low_one = lax.broadcasted_iota(jnp.int32, (1, LANES), 1) < 64
        extra_ref[...] = jnp.zeros_like(extra_ref)
        for share in range(4):

            @pl.when(shard_ref[0] == share)
            def _(share=share):
                odd = share % 2 == 1

                def tile(first, stride):
                    here = held[pl.ds(first, 8, stride=stride), :]
                    if not odd:
                        return here
                    ahead = held[pl.ds(first - 1, 8, stride=stride), :]
                    return jnp.where(low, pltpu.roll(ahead, 64, 1), pltpu.roll(here, 64, 1))

                for box, groups, box_row, flat_row, stride in block.parts(share):
                    base = MARGIN + block.start[share] + flat_row

                    def body(group, carry, box=box, base=base, box_row=box_row, stride=stride):
                        for j in range(6):
                            first = base + 16 * stride * group + j
                            both = jnp.concatenate([tile(first, stride), tile(first + 8 * stride, stride)], axis=0)
                            at = pl.multiple_of(box_row + 16 * group, 16)
                            box_refs[box][pl.ds(at, 16), LANES * j : LANES * j + LANES] = both.astype(BF)
                        return carry

                    lax.fori_loop(0, groups, body, 0, unroll=8)
                count = flat_rows(block, share)
                for to, row, length in block.extra[share]:
                    for k in range(length):
                        at = MARGIN + row + k
                        value = held[at : at + 1, :]
                        if odd:
                            ahead = held[at - 1 : at, :]
                            value = jnp.where(low_one, pltpu.roll(ahead, 64, 1), pltpu.roll(value, 64, 1))
                            if row + k == 0:
                                value = jnp.where(low_one, 0.0, value)
                        elif row + k == count:
                            value = jnp.where(low_one, value, 0.0)
                        extra_ref[to + k : to + k + 1, :] = value.astype(BF).astype(F32)


def flat_rows(block, share):
    return 4615 if block is ATTN else 9226


def prep(block, flat, shard):
    steps = -(-flat.shape[0] // (CHUNK * LANES))
    return pl.pallas_call(
        functools.partial(prep_kernel, block, steps),
        grid=(steps,),
        in_specs=[SMEM, pl.BlockSpec((CHUNK * LANES,), lambda i: (i,))],
        out_specs=[pl.BlockSpec((D, D), lambda i: (0, 0))] * block.boxes
        + [pl.BlockSpec((EXTRA, LANES), lambda i: (0, 0))],
        out_shape=[sds((D, D), BF)] * block.boxes + [sds((EXTRA, LANES), F32)],
        scratch_shapes=[pltpu.VMEM((MARGIN + CHUNK * steps + MARGIN, LANES), F32)],
        compiler_params=params(),
    )(shard, flat)


def spread_row(extra_ref, first, count):
    return jnp.concatenate([extra_ref[first + k : first + k + 1, :] for k in range(count)], axis=1)


def patch_row(ref, row, values):
    at = row // 16 * 16
    rows = lax.broadcasted_iota(jnp.int32, (16, values.shape[1]), 0)
    old = ref[at : at + 16, :].astype(F32)
    ref[at : at + 16, :] = jnp.where(rows == row - at, values, old).astype(BF)


def load_attn(shard, boxes, qkv_ref, proj_ref, sems):
    for wait in (False, True):
        for k, box in enumerate(boxes):
            share = jnp.bitwise_xor(shard, k)

            @pl.when(share == 3)
            def _(box=box, k=k):
                copy = pltpu.make_async_copy(box, proj_ref, sems.at[k, 0])
                copy.wait() if wait else copy.start()

            @pl.when(share != 3)
            def _(box=box, k=k, share=share):
                for part in range(3):
                    copy = pltpu.make_async_copy(
                        box.at[pl.ds(256 * part, 256), :],
                        qkv_ref.at[pl.ds(pl.multiple_of(768 * part + 256 * share, 256), 256), :],
                        sems.at[k, part],
                    )
                    copy.wait() if wait else copy.start()


def load_feed(shard, boxes, up_ref, down_ref, sems):
    for wait in (False, True):
        for k, box in enumerate(boxes):
            share = jnp.bitwise_xor(shard, k)

            @pl.when(share >= 2)
            def _(box=box, k=k, share=share):
                at = pl.multiple_of(768 * (share - 2), 256)
                copy = pltpu.make_async_copy(box, down_ref.at[pl.ds(at, 768), :], sems.at[k, 0])
                copy.wait() if wait else copy.start()

            @pl.when(share < 2)
            def _(box=box, k=k, share=share):
                for h in range(2):
                    copy = pltpu.make_async_copy(
                        box.at[pl.ds(384 * h, 384), :],
                        up_ref.at[pl.ds(pl.multiple_of(768 * h + 384 * share, 128), 384), :],
                        sems.at[k, h],
                    )
                    copy.wait() if wait else copy.start()


ANYWHERE = pl.BlockSpec(memory_space=pl.ANY)


def half_masks():
    lane = lax.broadcasted_iota(jnp.int32, (1, LANES), 1)
    return (lane < 64).astype(F32).astype(BF), (lane >= 64).astype(F32).astype(BF)


def two_heads(pair, masks):
    return jnp.concatenate([pair * masks[0], pair * masks[1]], axis=0)


def attn_forward(seq, x_ref, shard_ref, extra_ref, a0, a1, a2, a3, *refs):
    *refs, qkv_w, proj_w, vec_ref, bias_ref, sems = refs

    @pl.when(pl.program_id(0) == 0)
    def _():
        load_attn(shard_ref[0], (a0, a1, a2, a3), qkv_w, proj_w, sems)
        for part in range(3):
            patch_row(qkv_w, 768 * part + 255, spread_row(extra_ref, 12 + 6 * part, 6))
            patch_row(qkv_w, 768 * part + 512, spread_row(extra_ref, 30 + 6 * part, 6))
        vec_ref[...] = jnp.zeros_like(vec_ref)
        for row, first in enumerate((0, 6, 60, EXTRA + 0, EXTRA + 6)):
            vec_ref[row : row + 1, :] = spread_row(extra_ref, first, 6)
        bias_ref[...] = jnp.zeros_like(bias_ref)
        bias_ref[0:1, 0:768] = spread_row(extra_ref, 48, 6)
        bias_ref[0:1, 1536:2304] = spread_row(extra_ref, 54, 6)

    first_ref, qkv_ref, log_ref, att_ref, hid_ref, second_ref = refs
    x = x_ref[...].astype(F32)
    normed, _ = normed_of(x)
    first = (normed * vec_ref[0:1, :] + vec_ref[1:2, :]).astype(BF)
    first_ref[...] = first
    for part in range(3):
        cols = slice(768 * part, 768 * part + 768)
        qkv_ref[:, cols] = (dot(first, qkv_w[cols, :]) + bias_ref[0:1, cols]).astype(BF)
    masks = half_masks()
    real = lax.broadcasted_iota(jnp.int32, (2, T, T), 1) < seq
    for pair in range(HEADS // 2):
        at = LANES * pair
        q = qkv_ref[:, at : at + LANES] * jnp.asarray(0.125, BF)
        k = two_heads(qkv_ref[:, 768 + at : 768 + at + LANES], masks)
        v = two_heads(qkv_ref[:, 1536 + at : 1536 + at + LANES], masks)
        scores = dot_nt(k, q).reshape(2, T, T)
        scores = jnp.where(real, scores, -1e30)
        top = jnp.max(scores, axis=1, keepdims=True)
        weight = jnp.exp(scores - top)
        total = jnp.sum(weight, axis=1, keepdims=True)
        logs = top + jnp.log(total)
        log_ref[0, 2 * pair : 2 * pair + 1, :] = logs[0]
        log_ref[0, 2 * pair + 1 : 2 * pair + 2, :] = logs[1]
        probs = (weight * (1.0 / total)).astype(BF).reshape(2 * T, T)
        att_ref[:, at : at + LANES] = dot_tn(probs, v).astype(BF)
    hidden = x + dot(att_ref[...], proj_w[...]) + vec_ref[2:3, :]
    hid_ref[...] = hidden
    normed, _ = normed_of(hidden)
    second_ref[...] = (normed * vec_ref[3:4, :] + vec_ref[4:5, :]).astype(BF)


def call_attn_forward(seq, x, weights, boxes):
    shard, extra = weights
    rows = x.shape[0]
    images = rows // T
    made = [sds((2304, D), BF), sds((D, D), BF), sds((8, D), F32), sds((8, 2304), F32)]
    return pl.pallas_call(
        functools.partial(attn_forward, seq),
        grid=(images,),
        in_specs=[rows_of(T, D), SMEM, whole(extra)] + [ANYWHERE] * 4,
        out_specs=[
            rows_of(T, D),
            rows_of(T, 2304),
            pl.BlockSpec((1, HEADS, T), lambda i: (i, 0, 0)),
            rows_of(T, D),
            rows_of(T, D),
            rows_of(T, D),
        ]
        + [pl.BlockSpec(shape.shape, lambda i: (0, 0)) for shape in made],
        out_shape=[
            sds((rows, D), BF),
            sds((rows, 2304), BF),
            sds((images, HEADS, T), F32),
            sds((rows, D), BF),
            sds((rows, D), F32),
            sds((rows, D), BF),
        ]
        + made,
        scratch_shapes=[pltpu.SemaphoreType.DMA((4, 3))],
        compiler_params=params(),
    )(x, shard, extra, *boxes)


HALF = FF // 2
ROW_STEPS = 4


def feed(seq, part, tall, shard_ref, extra_ref, a0, a1, a2, a3, second_ref, cot_ref, result_ref, *refs):
    last = part == 1
    if last:
        before_ref, out_ref, gs_ref, *refs = refs
    else:
        out_ref, gs_ref, cot_sum, *refs = refs
    sum_ref, edge_ref, other_ref, mine_ref, up_w, down_w, bias, second_all, cot_all, act_all, pre_all, box, sems = refs
    step = pl.program_id(0)
    shard = shard_ref[0]

    @pl.when(step == 0)
    def _():
        load_feed(shard, (a0, a1, a2, a3), up_w, down_w, sems)
        for h in range(2):
            patch_row(up_w, 768 * h + 383, spread_row(extra_ref, EXTRA + 12 + 12 * h + 6 * part, 6))
            bias[0:1, 768 * h : 768 * h + 768] = spread_row(extra_ref, EXTRA + 36 + 12 * h + 6 * part, 6)
        if last:
            patch_row(down_w, 767, spread_row(extra_ref, EXTRA + 60, 6))
        sum_ref[...] = jnp.zeros_like(sum_ref)
        edge_ref[...] = jnp.zeros_like(edge_ref)
        if not last:
            cot_sum[...] = jnp.zeros_like(cot_sum)

    @pl.when(step < ROW_STEPS)
    def _():
        at = pl.ds(pl.multiple_of(step * tall, 16), tall)
        second = second_ref[...]
        cot = cot_ref[...]
        second_all[at, :] = second
        cot_all[at, :] = cot
        if last:
            result = result_ref[...]
            grad_second = before_ref[...]
        else:
            result = result_ref[...] + spread_row(extra_ref, EXTRA + 66, 6)
            grad_second = jnp.zeros_like(result)
            cot_sum[0:1, :] += jnp.sum(cot.astype(F32), axis=0, keepdims=True)
        for h in range(2):
            cols = slice(768 * h, 768 * h + 768)
            pre = dot(second, up_w[cols, :]) + bias[0:1, cols]
            grad_act = dot_nt(cot, down_w[cols, :])
            half = 0.5 * (1.0 + lax.erf(pre * root_half))
            act = (pre * half).astype(BF)
            grad_pre = grad_act * (half + pre * jnp.exp(-0.5 * pre * pre) * inv_root_tau)
            low = grad_pre.astype(BF)
            act_all[at, cols] = act
            pre_all[at, cols] = low
            sum_ref[0:1, cols] += jnp.sum(grad_pre, axis=0, keepdims=True)
            result = result + dot(act, down_w[cols, :])
            grad_second = grad_second + dot_nt(low, up_w[cols, :])
        if last:
            for image in range(tall // T):
                out_ref[image] = result[T * image : T * image + seq].astype(BF)
        else:
            out_ref[...] = result
        gs_ref[...] = grad_second

    index = step - ROW_STEPS
    side = jnp.bitwise_xor(shard // 2, index % 2)
    core = jnp.where(index >= 2, shard % 2, 1 - shard % 2)

    @pl.when((index >= 0) & (side == 0))
    def _():
        left = second_all[:, pl.ds(pl.multiple_of(384 * core, 128), 384)]
        for h in range(2):
            grad = dot_tn(left, pre_all[:, 768 * h : 768 * h + 768])
            box[384 * h : 384 * h + 384, :] = grad.astype(BF)

            @pl.when(core == 0)
            def _(grad=grad, h=h):
                edge_ref[0:1, 768 * h : 768 * h + 768] = grad[383:384]

    @pl.when((index >= 0) & (side == 1))
    def _():
        left = act_all[:, pl.ds(pl.multiple_of(768 * core, 128), 768)]
        grad = dot_tn(left, cot_all[...])
        box[...] = grad.astype(BF)

        @pl.when(core == 0)
        def _():
            edge_ref[1:2, 0:768] = grad[767:768]

    @pl.when((index >= 0) & (index < 2))
    def _():
        other_ref[0] = box[...]

    @pl.when(index >= 2)
    def _():
        mine_ref[0] = box[...]


def call_feed(seq, part, shard, extra, boxes, second, cot, result, before=None):
    rows = second.shape[0]
    images = rows // T
    tall = rows // ROW_STEPS
    last = part == 1
    row = lambda i: jnp.minimum(i, ROW_STEPS - 1)
    block = pl.BlockSpec((tall, D), lambda i: (row(i), 0))
    out = pl.BlockSpec((tall // T, seq, D), lambda i: (row(i), 0, 0)) if last else block
    grads = lambda first: pl.BlockSpec((1, D, D), lambda i: (jnp.clip(i - ROW_STEPS - first, 0, 1), 0, 0))
    small = lambda width: pl.BlockSpec((8, width), lambda i: (0, 0))
    return pl.pallas_call(
        functools.partial(feed, seq, part, tall),
        grid=(ROW_STEPS + 4,),
        in_specs=[SMEM, whole(extra)] + [ANYWHERE] * 4 + [block] * (4 if last else 3),
        out_specs=[out, block] + ([] if last else [small(D)]) + [small(HALF), small(HALF), grads(0), grads(2)],
        out_shape=[sds((images, seq, D), BF) if last else sds((rows, D), F32), sds((rows, D), F32)]
        + ([] if last else [sds((8, D), F32)])
        + [sds((8, HALF), F32), sds((8, HALF), F32), sds((2, D, D), BF), sds((2, D, D), BF)],
        scratch_shapes=[
            pltpu.VMEM((HALF, D), BF),
            pltpu.VMEM((HALF, D), BF),
            pltpu.VMEM((8, HALF), F32),
            pltpu.VMEM((rows, D), BF),
            pltpu.VMEM((rows, D), BF),
            pltpu.VMEM((rows, HALF), BF),
            pltpu.VMEM((rows, HALF), BF),
            pltpu.VMEM((D, D), BF),
            pltpu.SemaphoreType.DMA((4, 2)),
        ],
        compiler_params=params(60),
    )(shard, extra, *boxes, second, cot, result, *([before] if last else []))


WIDE = 384


def attn_backward(seq, images, group, shard_ref, log_ref, qkv_ref, first_ref, att_ref, *refs):
    step = pl.program_id(0)
    shard = shard_ref[0]
    if group == 0:
        gs_ref, hid_ref, cot_ref, vec_ref, proj_w, grad_ref, head_sum, low_ref, ga_ref, gh_ref, sum_ref, *refs = refs
    else:
        low_ref, ga_ref, grad_ref, head_sum, *refs = refs
    edge_ref, other_ref, mine_ref, grad_all, first_all, low_all, att_all, box = refs

    @pl.when(step == 0)
    def _():
        head_sum[...] = jnp.zeros_like(head_sum)
        edge_ref[...] = jnp.zeros_like(edge_ref)
        if group == 0:
            sum_ref[...] = jnp.zeros_like(sum_ref)

    @pl.when(step < images)
    def _():
        at_rows = pl.ds(pl.multiple_of(step * T, 16), T)
        first_all[at_rows, :] = first_ref[...]
        att_all[at_rows, :] = att_ref[...]
        if group == 0:
            gs = gs_ref[...]
            normed, spread = normed_of(hid_ref[...])
            gn = gs * vec_ref[3:4, :]
            gh = cot_ref[...].astype(F32) + spread * (
                gn - jnp.mean(gn, axis=-1, keepdims=True) - normed * jnp.mean(gn * normed, axis=-1, keepdims=True)
            )
            sum_ref[0:1, :] += jnp.sum(gs * normed, axis=0, keepdims=True)
            sum_ref[1:2, :] += jnp.sum(gs, axis=0, keepdims=True)
            sum_ref[2:3, :] += jnp.sum(gh, axis=0, keepdims=True)
            gh_ref[...] = gh
            gh_low = gh.astype(BF)
            low_ref[...] = gh_low
            ga_ref[...] = dot_nt(gh_low, proj_w[...]).astype(BF)
        low_all[at_rows, :] = low_ref[...]
        low = lax.broadcasted_iota(jnp.int32, (T, LANES), 1) < 64
        real = lax.broadcasted_iota(jnp.int32, (2, T, T), 1) < seq
        eighth = jnp.asarray(0.125, BF)
        masks = half_masks()
        for pair in range(3):
            at = LANES * pair
            full = WIDE * group + at
            head = 6 * group + 2 * pair
            q = qkv_ref[:, full : full + LANES] * eighth
            k = two_heads(qkv_ref[:, 768 + full : 768 + full + LANES], masks)
            v = two_heads(qkv_ref[:, 1536 + full : 1536 + full + LANES], masks)
            grad_out = ga_ref[:, at : at + LANES]
            scores = dot_nt(k, q).reshape(2, T, T)
            logs = jnp.concatenate([log_ref[0:1, head : head + 1, :], log_ref[0:1, head + 1 : head + 2, :]], axis=0)
            probs = jnp.where(real, jnp.exp(scores - logs), 0.0)
            grad_v = dot(probs.astype(BF).reshape(2 * T, T), grad_out)
            grad_probs = dot_nt(v, grad_out).reshape(2, T, T)
            delta = jnp.sum(probs * grad_probs, axis=1, keepdims=True)
            grad_scores = (probs * (grad_probs - delta)).astype(BF).reshape(2 * T, T)
            grad_k = dot(grad_scores, q)
            grads = (
                dot_tn(grad_scores, k * eighth),
                jnp.where(low, grad_k[:T], grad_k[T:]),
                jnp.where(low, grad_v[:T], grad_v[T:]),
            )
            for part, grad in enumerate(grads):
                if part != 1:
                    row = part // 2
                    head_sum[row : row + 1, at : at + LANES] += jnp.sum(grad, axis=0, keepdims=True)
                cols = slice(WIDE * part + at, WIDE * part + at + LANES)
                grad = grad.astype(BF)
                grad_ref[:, cols] = grad
                grad_all[at_rows, cols] = grad

    index = step - images
    side = jnp.bitwise_xor(shard // 2, index % 2)
    core = jnp.where(index >= 2, shard % 2, 1 - shard % 2)
    share = 2 * side + core

    @pl.when((index >= 0) & (share == 3))
    def _():
        box[...] = dot_tn(att_all[...], low_all[...]).astype(BF)

    @pl.when((index >= 0) & (share != 3))
    def _():
        grad = dot_tn(first_all[:, pl.ds(pl.multiple_of(256 * share, 256), 256)], grad_all[...])
        for part in range(3):
            cols = slice(WIDE * part, WIDE * part + WIDE)
            for u in range(2):
                box[128 * part : 128 * part + 128, WIDE * u : WIDE * u + WIDE] = grad[
                    128 * u : 128 * u + 128, cols
                ].astype(BF)

        @pl.when(share == 0)
        def _():
            edge_ref[0:1, :] = grad[255:256]

        @pl.when(share == 2)
        def _():
            edge_ref[1:2, :] = grad[0:1]

    @pl.when((index >= 0) & (index < 2))
    def _():
        other_ref[0] = box[...]

    @pl.when(index >= 2)
    def _():
        mine_ref[0] = box[...]


def call_attn_backward(seq, group, shard, log_total, qkv, first, attended, *more):
    rows = first.shape[0]
    images = rows // T
    row = lambda i: jnp.minimum(i, images - 1)
    block = lambda width, col=0: pl.BlockSpec((T, width), lambda i: (row(i), col))
    small = lambda width: pl.BlockSpec((8, width), lambda i: (0, 0))
    grads = lambda at: pl.BlockSpec((1, WIDE, D), lambda i: (jnp.clip(i - images - at, 0, 1), 0, 0))
    in_specs = [SMEM, pl.BlockSpec((1, HEADS, T), lambda i: (row(i), 0, 0)), block(2304), block(D), block(WIDE, group)]
    out_specs = [block(3 * WIDE), small(WIDE)]
    out_shape = [sds((rows, 3 * WIDE), BF), sds((8, WIDE), F32)]
    if group == 0:
        in_specs += [block(D)] * 3 + [whole(more[3]), whole(more[4])]
        out_specs += [block(D), block(D), block(D), small(D)]
        out_shape += [sds((rows, D), BF), sds((rows, D), BF), sds((rows, D), F32), sds((8, D), F32)]
    else:
        in_specs += [block(D), block(WIDE, 1)]
    return pl.pallas_call(
        functools.partial(attn_backward, seq, images, group),
        grid=(images + 4,),
        in_specs=in_specs,
        out_specs=out_specs + [small(3 * WIDE), grads(0), grads(2)],
        out_shape=out_shape + [sds((8, 3 * WIDE), F32), sds((2, WIDE, D), BF), sds((2, WIDE, D), BF)],
        scratch_shapes=[
            pltpu.VMEM((rows, 3 * WIDE), BF),
            pltpu.VMEM((rows, D), BF),
            pltpu.VMEM((rows, D), BF),
            pltpu.VMEM((rows, WIDE), BF),
            pltpu.VMEM((WIDE, D), BF),
        ],
        compiler_params=params(),
    )(shard, log_total, qkv, first, attended, *more)


def input_backward(seq, grad0, grad1, gh_ref, x_ref, vec_ref, qkv_w, out_ref, sum_ref):
    @pl.when(pl.program_id(0) == 0)
    def _():
        sum_ref[...] = jnp.zeros_like(sum_ref)

    grad_first = None
    for part in range(3):
        cols = slice(WIDE * part, WIDE * part + WIDE)
        both = jnp.concatenate([grad0[:, cols], grad1[:, cols]], axis=1)
        term = dot_nt(both, qkv_w[768 * part : 768 * part + 768, :])
        grad_first = term if part == 0 else grad_first + term
    normed, spread = normed_of(x_ref[...].astype(F32))
    gn = grad_first * vec_ref[0:1, :]
    grad = gh_ref[...] + spread * (
        gn - jnp.mean(gn, axis=-1, keepdims=True) - normed * jnp.mean(gn * normed, axis=-1, keepdims=True)
    )
    sum_ref[0:1, :] += jnp.sum(grad_first * normed, axis=0, keepdims=True)
    sum_ref[1:2, :] += jnp.sum(grad_first, axis=0, keepdims=True)
    for image in range(grad.shape[0] // T):
        out_ref[image] = grad[T * image : T * image + seq].astype(BF)


def call_input_backward(seq, grads, gh, x, vec, qkv_w):
    rows = gh.shape[0]
    images = rows // T
    step = 2 if images % 2 == 0 else 1
    tall = step * T
    return pl.pallas_call(
        functools.partial(input_backward, seq),
        grid=(images // step,),
        in_specs=[rows_of(tall, 3 * WIDE)] * 2 + [rows_of(tall, D), rows_of(tall, D), whole(vec), whole(qkv_w)],
        out_specs=[pl.BlockSpec((step, seq, D), lambda i: (i, 0, 0)), pl.BlockSpec((8, D), lambda i: (0, 0))],
        out_shape=[sds((images, seq, D), BF), sds((8, D), F32)],
        compiler_params=params(),
    )(*grads, gh, x, vec, qkv_w)


def pack(last_sum, back_sum, head0, head1, edge0, edge1, pre0, pre1, up0, up1, cot_sum, out_ref):
    out_ref[...] = jnp.zeros_like(out_ref)

    def put(first, ref, row, col, width):
        for k in range(width // LANES):
            at = col + LANES * k
            out_ref[first + k : first + k + 1, :] = ref[row : row + 1, at : at + LANES]

    put(0, last_sum, 0, 0, D)
    put(6, last_sum, 1, 0, D)
    for group, (head, edge) in enumerate(((head0, edge0), (head1, edge1))):
        for part in range(3):
            put(12 + 6 * part + 3 * group, edge, 0, WIDE * part, WIDE)
            put(30 + 6 * part + 3 * group, edge, 1, WIDE * part, WIDE)
        put(48 + 3 * group, head, 0, 0, WIDE)
        put(54 + 3 * group, head, 1, 0, WIDE)
    put(60, back_sum, 2, 0, D)
    put(EXTRA, back_sum, 0, 0, D)
    put(EXTRA + 6, back_sum, 1, 0, D)
    for j, (pre, up) in enumerate(((pre0, up0), (pre1, up1))):
        for h in range(2):
            put(EXTRA + 12 + 12 * h + 6 * j, up, 0, 768 * h, D)
            put(EXTRA + 36 + 12 * h + 6 * j, pre, 0, 768 * h, D)
    put(EXTRA + 60, up1, 1, 0, D)
    put(EXTRA + 66, cot_sum, 0, 0, D)


def call_pack(*arrays):
    return pl.pallas_call(
        pack,
        in_specs=[pl.BlockSpec(memory_space=pltpu.VMEM)] * len(arrays),
        out_specs=pl.BlockSpec(memory_space=pltpu.VMEM),
        out_shape=sds((2 * EXTRA, LANES), F32),
        compiler_params=params(),
    )(*arrays)


def adam_kernel(block, share_size, scale, boxes, shard_ref, power_ref, extra_ref, *refs):
    box_refs = refs[:boxes]
    flat_ref, mom_ref, grad_ref, change_ref, new_ref, held = refs[boxes:]
    step = pl.program_id(0)

    @pl.when(step == 0)
    def _():
        for share in range(4):

            @pl.when(shard_ref[0] == share)
            def _(share=share):
                for box, groups, box_row, col, cols, flat_row, stride in block.grad_parts(share):
                    base = MARGIN + block.start[share] + flat_row

                    def body(group, carry, box=box, box_row=box_row, col=col, cols=cols, base=base, stride=stride):
                        row = pl.multiple_of(box_row + 16 * group, 16)
                        for j in range(cols):
                            at = LANES * (col + j)
                            both = box_refs[box][pl.ds(row, 16), at : at + LANES].astype(F32)
                            to = base + 16 * stride * group + j
                            held[pl.ds(to, 8, stride=stride), :] = both[0:8]
                            held[pl.ds(to + 8 * stride, 8, stride=stride), :] = both[8:16]
                        return carry

                    lax.fori_loop(0, groups, body, 0, unroll=8)
                for source, row, length in block.put[share]:
                    held[MARGIN + row : MARGIN + row + length, :] = extra_ref[block.base + source : block.base + source + length, :]

    start = pl.multiple_of(MARGIN + CHUNK * step, 8)
    shard = shard_ref[0]
    low = lax.broadcasted_iota(jnp.int32, (CHUNK, LANES), 1) < 64
    here = held[pl.ds(start, CHUNK), :]
    after = held[pl.ds(start + 1, CHUNK), :]
    shifted = jnp.where(low, pltpu.roll(here, 64, 1), pltpu.roll(after, 64, 1))
    grad = jnp.where(shard % 2 == 1, shifted, here) * scale
    position = (
        shard * share_size
        + step * (CHUNK * LANES)
        + lax.broadcasted_iota(jnp.int32, (CHUNK, LANES), 0) * LANES
        + lax.broadcasted_iota(jnp.int32, (CHUNK, LANES), 1)
    )
    matrix = jnp.zeros((CHUNK, LANES), jnp.bool_)
    for first, end in block.matrices:
        matrix = matrix | ((position >= first) & (position < end))
    size = CHUNK * LANES
    p = flat_ref[...].reshape(CHUNK, LANES)
    m = beta_one * mom_ref[0, :].reshape(CHUNK, LANES) + (1.0 - beta_one) * grad
    s = beta_two * mom_ref[1, :].reshape(CHUNK, LANES) + (1.0 - beta_two) * grad * grad
    ratio = (m * power_ref[0]) / (jnp.sqrt(s * power_ref[1]) + adam_eps)
    change = jnp.where(matrix, rate_matrix, rate_vector) * (ratio + jnp.where(matrix, decay_matrix, 0.0) * p)
    grad_ref[...] = grad.reshape(size)
    change_ref[...] = change.reshape(size)
    new_ref[0, :] = m.reshape(size)
    new_ref[1, :] = s.reshape(size)


def adam(block, shard, powers, extra, boxes, flat, moments, scale):
    count = flat.shape[0]
    steps = -(-count // (CHUNK * LANES))
    line = pl.BlockSpec((CHUNK * LANES,), lambda i: (i,))
    two = pl.BlockSpec((2, CHUNK * LANES), lambda i: (0, i))
    return pl.pallas_call(
        functools.partial(adam_kernel, block, count, scale, len(boxes)),
        grid=(steps,),
        in_specs=[SMEM, SMEM, whole(extra)] + [whole(box) for box in boxes] + [line, two],
        out_specs=[line, line, two],
        out_shape=[sds((count,), F32), sds((count,), F32), sds((2, count), F32)],
        scratch_shapes=[pltpu.VMEM((MARGIN + CHUNK * steps + MARGIN, LANES), F32)],
        compiler_params=params(),
    )(shard, powers, extra, *boxes, flat, moments)


def swap(value, axis, bit):
    pairs = [(i, i ^ bit) for i in range(lax.axis_size(axis))]
    return lax.ppermute(value, axis, pairs)


def turn(value, axis, unit, distance):
    size = lax.axis_size(axis)
    return lax.ppermute(value, axis, [(i, (i + unit * distance) % size) for i in range(size)])


def pick(array, index, axis=0):
    return lax.dynamic_index_in_dim(array, index, axis, keepdims=False)


class Line:
    def __init__(self):
        self.last = None

    def __call__(self, step, *args):
        if self.last is not None:
            flat, tree = jax.tree.flatten(args)
            flat = lax.optimization_barrier((self.last, *flat))[1:]
            args = jax.tree.unflatten(tree, flat)
        out = step(*args)
        self.last = min(jax.tree.leaves(out), key=lambda leaf: leaf.size)
        return out


class Sum:
    def __init__(self, line, mine, other):
        self.line, self.mine = line, mine
        self.rows = mine.shape[1]
        rep = lax.axis_index("rep")
        self.near, self.far = rep % 2, rep // 2
        self.count = lax.axis_size("rep") // 2
        self.came = swap(other, "shard", 1)

    def side(self):
        send = self.line(lambda m, c: (m.astype(F32) + c.astype(F32)).astype(BF), self.mine[1], self.came[1])
        self.mine, self.here = self.mine[0], self.came[0]
        self.came = swap(send, "shard", 2)

    def close(self):
        def step(mine, here, came):
            total = mine.astype(F32) + here.astype(F32) + came.astype(F32)
            halves = total.reshape(2, self.rows // 2, D)
            return pick(halves, 1 - self.near).astype(BF), pick(halves, self.near)

        send, self.half = self.line(step, self.mine, self.here, self.came)
        self.came = swap(send, "rep", 1)

    def along(self):
        def step(half, came):
            parts = (half + came.astype(F32)).reshape(self.count, self.rows // 2 // self.count, D)
            sends = [pick(parts, (self.far + d) % self.count).astype(BF) for d in range(1, self.count)]
            return sends, pick(parts, self.far)

        sends, self.part = self.line(step, self.half, self.came)
        self.came = [turn(send, "rep", 2, d + 1) for d, send in enumerate(sends)]

    def back_along(self):
        def step(part, came):
            for value in came:
                part = part + value.astype(F32)
            return part.astype(BF)

        self.part = self.line(step, self.part, self.came)
        self.came = [turn(self.part, "rep", 2, d) for d in range(1, self.count)]

    def back_close(self):
        def step(part, came):
            full = jnp.zeros((self.count,) + part.shape, BF)
            for d, value in enumerate([part] + came):
                full = lax.dynamic_update_slice_in_dim(full, value[None], (self.far + self.count - d) % self.count, 0)
            return full.reshape(self.rows // 2, D)

        self.half = self.line(step, self.part, self.came)
        self.came = swap(self.half, "rep", 1)

    def end(self):
        def step(half, came):
            first = self.near == 0
            return jnp.concatenate([jnp.where(first, half, came), jnp.where(first, came, half)], axis=0)

        return self.line(step, self.half, self.came)


class SumAll:
    def __init__(self, line, value):
        self.line, self.value = line, value
        self.hops = [("shard", 1), ("shard", 2)]
        bit = 1
        while bit < lax.axis_size("rep"):
            self.hops.append(("rep", bit))
            bit *= 2
        self.came = swap(value, *self.hops.pop(0))

    def hop(self):
        self.value = self.line(lambda a, b: a + b, self.value, self.came)
        if self.hops:
            self.came = swap(self.value, *self.hops.pop(0))
            return False
        return True


def body(layer_input, out_cotangent, attention_params, attention_moments, feedforward_params, feedforward_moments, step_count):
    images, seq, _ = layer_input.shape
    rows = images * T
    image_total = images * lax.axis_size("shard") * lax.axis_size("rep")
    scale = 1.0 / image_total
    shard = lax.axis_index("shard").astype(jnp.int32).reshape(1)
    time = step_count[0].astype(F32)
    powers = jnp.stack([1.0 / (1.0 - jnp.power(beta_one, time)), 1.0 / (1.0 - jnp.power(beta_two, time))])
    pad = ((0, 0), (0, T - seq), (0, 0))
    padded = lambda tokens: jnp.pad(tokens, pad).reshape(rows, D)
    line = Line()

    attn_box, attn_extra = line(functools.partial(prep, ATTN), attention_params, shard)
    attn_across = swap(attn_box, "shard", 2)
    attn_near = swap(attn_box, "shard", 1)
    box0, box1, feed_extra = line(functools.partial(prep, FEED), feedforward_params, shard)
    extra = line(lambda a, b: jnp.concatenate([a, b], axis=0), attn_extra, feed_extra)
    came = swap(extra, "shard", 1)
    x = line(padded, layer_input)
    extra = line(lambda a, b: a + b, extra, came)
    came = swap(extra, "shard", 2)
    cot = line(padded, out_cotangent)
    extra = line(lambda a, b: a + b, extra, came)
    near0, near1 = swap(box0, "shard", 1), swap(box1, "shard", 1)
    across, send0 = line(lambda a, b: lax.optimization_barrier((a, b)), attn_across, box0)
    attn_both = swap(across, "shard", 1)
    across0 = swap(send0, "shard", 2)
    boxes = (attn_box, attn_near, attn_across, attn_both)
    first, qkv, log_total, attended, hidden, second, qkv_w, proj_w, vec, bias = line(
        lambda x, w, b: call_attn_forward(seq, x, w, b), x, (shard, extra), boxes
    )
    across, send1 = line(lambda a, b: lax.optimization_barrier((a, b)), across0, box1)
    both0 = swap(across, "shard", 1)
    across1 = swap(send1, "shard", 2)
    boxes = (box0, near0, across0, both0)
    result, gs, cot_sum, pre0, up0, other0, mine0 = line(
        lambda *a: call_feed(seq, 0, *a), shard, extra, boxes, second, cot, hidden
    )
    both1 = swap(line(lambda a: a, across1), "shard", 1)
    feed0 = Sum(line, mine0, other0)
    feed0.side()
    boxes = (box1, near1, across1, both1)
    layer_output, gs, pre1, up1, other1, mine1 = line(
        lambda *a: call_feed(seq, 1, *a), shard, extra, boxes, second, cot, result, gs
    )
    feed1 = Sum(line, mine1, other1)
    feed0.close()
    feed1.side()
    grad0, head0, gh_low, ga, gh, back_sum, edge0, other2, mine2 = line(
        lambda *a: call_attn_backward(seq, 0, *a), shard, log_total, qkv, first, attended, gs, hidden, cot, vec, proj_w
    )
    attn0 = Sum(line, mine2, other2)
    feed0.along()
    feed1.close()
    attn0.side()
    grad1, head1, edge1, other3, mine3 = line(
        lambda *a: call_attn_backward(seq, 1, *a), shard, log_total, qkv, first, attended, gh_low, ga
    )
    attn1 = Sum(line, mine3, other3)
    feed0.back_along()
    feed1.along()
    attn1.side()
    attn0.close()
    input_grad, last_sum = line(lambda *a: call_input_backward(seq, *a), (grad0, grad1), gh, x, vec, qkv_w)
    sums = line(call_pack, last_sum, back_sum, head0, head1, edge0, edge1, pre0, pre1, up0, up1, cot_sum)
    sums = SumAll(line, sums)
    feed0.back_close()
    feed1.back_along()
    attn0.along()
    sums.hop()
    attn1.close()
    sums.hop()
    feed1.back_close()
    attn0.back_along()
    attn1.along()
    sums.hop()
    feed_box0 = feed0.end()
    while not sums.hop():
        pass
    attn0.back_close()
    attn1.back_along()
    feed_box1 = feed1.end()
    attn_box0 = attn0.end()
    attn1.back_close()
    feed_grad, feed_change, feed_new = line(
        lambda *a: adam(FEED, *a, scale), shard, powers, sums.value, [feed_box0, feed_box1], feedforward_params, feedforward_moments
    )
    attn_grad, attn_change, attn_new = line(
        lambda *a: adam(ATTN, *a, scale), shard, powers, sums.value, [attn_box0, attn1.end()], attention_params, attention_moments
    )
    return (layer_output, input_grad, attn_grad, feed_grad, attn_change, attn_new, feed_change, feed_new)


def solution(mesh):
    tokens = P(("shard", "rep"), None, None)
    in_specs = (tokens, tokens, P("shard"), P(None, "shard"), P("shard"), P(None, "shard"), P())
    out_specs = (tokens, tokens, P("shard"), P("shard"), P("shard"), P(None, "shard"), P("shard"), P(None, "shard"))
    return jax.shard_map(body, mesh=mesh, in_specs=in_specs, out_specs=out_specs, check_vma=False)
```

profile of v0, /device:TPU:0, one launch (start us, length us, event | category | flops | bytes accessed | tf_op | source)
XLA Modules:
  0.0 413.9 jit_solution(4668296042375018838)
XLA Ops:
  0.6 3.0 shard_map.134
  3.6 3.0 collective-permute-start.2
  6.6 5.7 %shard_map.135 = (bf16[768,768]{1,0:T(8,128)(2,1)}, bf16[768,768]{1,0:T(8,128)(2,1)}, f32[72,128]{1,0:T(8,128)}) custom-call(s32[1]{0:T(128)} %bitcast.shard_ref, f32[1180992]{0:T(1024)} %refs_2_), custom_call_target="tpu_custom_call" | custom-call | tf_op jit(solution)/shard_map/pallas_call | solution.py:203
  13.1 1.6 collective-permute-start
  15.2 1.6 pad.7.clone
  18.6 1.6 pad.8.clone
  20.2 15.0 %collective-permute-done.1 = f32[144,128]{1,0:T(8,128)S(1)} collective-permute-done((f32[144,128]{1,0:T(8,128)S(1)}, f32[144,128]{1,0:T(8,128)S(1)}, u32[]{:S(2)}, u32[]{:S(2)}) %collective-permute-start.1) | collective-permute-done | bytes 73760 | tf_op jit(solution)/shard_map/ppermute | solution.py:778
  36.0 1.7 collective-permute-start.5
  39.9 29.6 %shard_map.136 = (bf16[1664,768]{1,0:T(8,128)(2,1)}, bf16[1664,2304]{1,0:T(8,128)(2,1)}, f32[8,12,208]{2,1,0:T(8,128)}, bf16[1664,768]{1,0:T(8,128)(2,1)}, f32[1...) custom-call(bf16[1664,768]{1,0:T(8,128)(2,1)} %bitcast.130, ...), custom_call_target="tpu_custom_call" | custom-call | tf_op jit(solution)/shard_map/pallas_call | solution.py:333
  69.9 2.5 collective-permute-done.7.a3
  73.5 36.9 %shard_map.137 = (f32[1664,768]{1,0:T(8,128)}, f32[1664,768]{1,0:T(8,128)}, f32[8,768]{1,0:T(8,128)}, f32[8,1536]{1,0:T(8,128)}, f32[8,1536]{1,0:T(8,128)}, /*in...) custom-call(s32[1]{0:T(128)} %bitcast.shard_ref, f32[144,128]{1,0:T(8,128)} %add.256.extra_ref, ...), custom_call_target="tpu_custom_call" | custom-call | tf_op jit(solution)/shard_map/pallas_call | solution.py:465
  110.7 1.4 collective-permute-start.8
  112.2 26.6 %collective-permute-done.8.a2 = bf16[768,768]{1,0:T(8,128)(2,1)S(1)} collective-permute-done((bf16[768,768]{1,0:T(8,128)(2,1)S(1)}, bf16[768,768]{1,0:T(8,128)(2,1)S(1)}, u32[]{:S(2)}, u32[]{:S(2)}) %collective-permute-start.8) | collective-permute-done | bytes 1179680 | tf_op jit(solution)/shard_map/ppermute | solution.py:778
  138.8 3.3 slice_bitcast_fusion.6
  142.1 1.2 slice_bitcast_fusion.2
  145.7 36.9 %shard_map.138 = (bf16[8,197,768]{2,1,0:T(8,128)(2,1)}, f32[1664,768]{1,0:T(8,128)}, f32[8,1536]{1,0:T(8,128)}, f32[8,1536]{1,0:T(8,128)}, bf16[2,768,768]{2,1,0:T(8,128)(2,1)}, /*index=5*/bf16[2,768,768]{2,1,0:T(8,128)(2,1)}) custom-call(s32[1]{0:T(128)} %bitcast.shard_ref, f32[144,128]{1,0:T(8,128)} %add.256.extra_ref, ...), custom_call_target="tpu_custom_call" | custom-call | tf_op jit(solution)/shard_map/pallas_call | solution.py:465
  182.7 1.5 collective-permute-start.12
  184.2 1.9 slice_bitcast_fusion.4
  186.1 24.9 %collective-permute-done.12 = bf16[768,768]{1,0:T(8,128)(2,1)S(1)} collective-permute-done((bf16[768,768]{1,0:T(8,128)(2,1)S(1)}, bf16[768,768]{1,0:T(8,128)(2,1)S(1)}, u32[]{:S(2)}, u32[]{:S(2)}) %collective-permute-start.12) | collective-permute-done | bytes 1179680 | tf_op jit(solution)/shard_map/ppermute | solution.py:778
  212.1 1.8 convert_add_fusion.1
  214.8 2.8 slice_bitcast_fusion
  217.6 1.3 add_convert_fusion
  218.9 1.5 collective-permute-start.15
  220.4 1.5 collective-permute-start.14
  221.9 30.6 %shard_map.139 = (bf16[1664,1152]{1,0:T(8,128)(2,1)}, f32[8,384]{1,0:T(8,128)}, bf16[1664,768]{1,0:T(8,128)(2,1)}, bf16[1664,768]{1,0:T(8,128)(2,1)}, f32[1664,7...) custom-call(s32[1]{0:T(128)} %bitcast.shard_ref, ...), custom_call_target="tpu_custom_call" | custom-call | tf_op jit(solution)/shard_map/pallas_call | solution.py:613
  252.7 1.2 convert_add_fusion.5
  254.7 1.6 collective-permute-start.17
  256.2 2.6 collective-permute-start.18
  258.8 1.3 collective-permute-start.19
  260.2 1.7 convert_add_fusion
  264.4 23.0 %shard_map.140 = (bf16[1664,1152]{1,0:T(8,128)(2,1)}, f32[8,384]{1,0:T(8,128)}, f32[8,1152]{1,0:T(8,128)}, bf16[2,384,768]{2,1,0:T(8,128)(2,1)}, bf16[2,384,768]{2,1,0:T(8,128)(2,1)}) custom-call(s32[1]{0:T(128)} %bitcast.shard_ref, f32[8,12,208]{2,1,0:T(8,128)} %get-tuple-element.326.log_ref, bf16[1664,2304]{1,0:T(8,128)(2,1)} %get-tuple-element.327.qkv_ref, ...), custom_call_target="tpu_custom_call" | custom-call | tf_op jit(solution)/shard_map/pallas_call | solution.py:613
  289.9 2.8 collective-permute-start.25
  294.8 1.5 collective-permute-start.27
  296.3 1.3 convert_add_fusion.3
  297.6 13.3 %shard_map.141 = (bf16[8,197,768]{2,1,0:T(8,128)(2,1)}, f32[8,768]{1,0:T(8,128)}) custom-call(bf16[1664,1152]{1,0:T(8,128)(2,1)} %get-tuple-element.350.grad0, bf16[1664,1152]{1,0:T(8,128)(2,1)} %get-tuple-element.351.grad1, f32[1664,768]{1,0:T(8,128)} %get-tuple-element.352.gh_ref, bf16[1664,768]{1,0:T(8,128)(2,1)} %bitcast.131, ...), custom_call_target="tpu_custom_call" | custom-call | tf_op jit(solution)/shard_map/pallas_call | solution.py:657
  310.9 1.7 shard_map.142
  312.6 2.9 collective-permute-start.28
  315.5 1.5 collective-permute-start.29
  319.0 1.5 collective-permute-start.31
  320.6 2.5 collective-permute-start.34
  323.3 1.3 collective-permute-start.35
  325.3 9.5 %collective-permute-done.31 = bf16[384,768]{1,0:T(8,128)(2,1)S(1)} collective-permute-done((bf16[384,768]{1,0:T(8,128)(2,1)S(1)}, bf16[384,768]{1,0:T(8,128)(2,1)S(1)}, u32[]{:S(2)}, u32[]{:S(2)}) %collective-permute-start.31) | collective-permute-done | bytes 589856 | tf_op jit(solution)/shard_map/ppermute | solution.py:778
  334.8 1.4 collective-permute-start.32
  336.4 2.7 collective-permute-done.32
  340.1 3.0 collective-permute-start.38
  343.8 1.9 collective-permute-done.36
  347.2 1.4 collective-permute-start.44
  348.6 1.3 collective-permute-start.45
  350.0 1.2 collective-permute-done.39
  352.5 1.5 collective-permute-start.42
  355.2 1.8 collective-permute-done.42
  356.9 2.0 collective-permute-start.43
  358.9 3.3 collective-permute-done.43
  362.3 1.4 collective-permute-start.47
  364.3 3.1 collective-permute-start.48
  368.3 1.9 collective-permute-start.51
  370.3 3.1 collective-permute-done.49
  374.0 1.9 collective-permute-start.53
  375.9 1.4 collective-permute-start.54
  380.9 1.8 collective-permute-start.55
  384.1 1.9 copy.17
  386.5 1.9 copy.18
  388.4 15.9 %shard_map.143 = (f32[1180992]{0:T(1024)}, f32[1180992]{0:T(1024)}, f32[2,1180992]{1,0:T(2,128)}) custom-call(s32[1]{0:T(128)} %bitcast.shard_ref, f32[2]{0:T(128)} %pad_maximum_fusion.4.power_ref, f32[144,128]{1,0:T(8,128)} %add.301.extra_ref, bf16[768,768]{1,0:T(8,128)(2,1)} %pad_maximum_fusion.refs_0_, bf16[768,768]{1,0:T(8,128)(2,1)} %pad_maximum_fusion.1.refs_1_, ...), custom_call_target="tpu_custom_call" | custom-call | tf_op jit(solution)/shard_map/pallas_call | solution.py:765
  405.2 8.2 %shard_map.144 = (f32[590784]{0:T(1024)}, f32[590784]{0:T(1024)}, f32[2,590784]{1,0:T(2,128)}) custom-call(s32[1]{0:T(128)} %bitcast.shard_ref, f32[2]{0:T(128)} %pad_maximum_fusion.4.power_ref, f32[144,128]{1,0:T(8,128)} %add.301.extra_ref, bf16[384,768]{1,0:T(8,128)(2,1)} %pad_maximum_fusion.2.refs_0_, bf16[384,768]{1,0:T(8,128)(2,1)} %pad_maximum_fusion.3.refs_1_, ...), custom_call_target="tpu_custom_call" | custom-call | tf_op jit(solution)/shard_map/pallas_call | solution.py:765
  (190 shorter events, 36.9 us)
Async XLA Ops:
  3.6 32.2 %collective-permute-start.2 = (bf16[768,768]{1,0:T(8,128)(2,1)}, bf16[768,768]{1,0:T(8,128)(2,1)S(1)}, u32[]{:S(2)}, u32[]{:S(2)}) collective-permute-start(bf16[768,768]{1,0:T(8,128)(2,1)} %get-tuple-element.248.a0), channel_id=1, source_target_pairs={{0,16},{8,24},{16,0},{24,8},{1,17},{9,25},{17,1},{25,9},{2,18},{10... | collective-permute-start | bytes 3538952 | tf_op jit(solution)/shard_map/ppermute | solution.py:778
  6.6 5.7 %copy-start.23 = (f32[72,128]{1,0:T(8,128)S(1)}, f32[72,128]{1,0:T(8,128)}, u32[]{:S(2)}) copy-start(f32[72,128]{1,0:T(8,128)} %get-tuple-element.232) | copy-start | bytes 110596
  6.6 8.1 %copy-start.5 = (bf16[8,197,768]{2,0,1:T(8,128)(2,1)S(1)}, bf16[8,197,768]{2,0,1:T(8,128)(2,1)}, u32[]{:S(2)}) copy-start(bf16[8,197,768]{2,0,1:T(8,128)(2,1)} %param.7) | copy-start | bytes 7262212
  13.1 3.7 collective-permute-start
  16.8 18.4 %collective-permute-start.1 = (f32[144,128]{1,0:T(8,128)S(1)}, f32[144,128]{1,0:T(8,128)S(1)}, u32[]{:S(2)}, u32[]{:S(2)}) collective-permute-start(f32[144,128]{1,0:T(8,128)S(1)} %add.255), channel_id=1, source_target_pairs={{0,16},{8,24},{16,0},{24,8},{1,17},{9,25},{17,1},{25,9},{2,18},{10... | collective-permute-start | bytes 221192 | tf_op jit(solution)/shard_map/ppermute | solution.py:778
  17.2 20.7 %collective-permute-start.3 = (bf16[768,768]{1,0:T(8,128)(2,1)S(1)}, bf16[768,768]{1,0:T(8,128)(2,1)S(1)}, u32[]{:S(2)}, u32[]{:S(2)}) collective-permute-start(bf16[768,768]{1,0:T(8,128)(2,1)S(1)} %copy-done.8), channel_id=1, source_target_pairs={{0,8},{8,0},{16,24},{24,16},{1,9},{9,1},{17,25},{25,17},{2,10},{10... | collective-permute-start | bytes 3538952 | tf_op jit(solution)/shard_map/ppermute | solution.py:778
  18.6 17.4 %copy-start.15 = (bf16[768,768]{1,0:T(8,128)(2,1)S(1)}, bf16[768,768]{1,0:T(8,128)(2,1)}, u32[]{:S(2)}) copy-start(bf16[768,768]{1,0:T(8,128)(2,1)} %get-tuple-element.262.a0) | copy-start | bytes 3538948
  35.9 2.8 collective-permute-start.4
  36.0 33.5 %collective-permute-start.5 = (bf16[768,768]{1,0:T(8,128)(2,1)S(1)}, bf16[768,768]{1,0:T(8,128)(2,1)S(1)}, u32[]{:S(2)}, u32[]{:S(2)}) collective-permute-start(bf16[768,768]{1,0:T(8,128)(2,1)S(1)} %copy-done.15), channel_id=1, source_target_pairs={{0,16},{8,24},{16,0},{24,8},{1,17},{9,25},{17,1},{25,9},{2,18},{10... | collective-permute-start | bytes 3538952 | tf_op jit(solution)/shard_map/ppermute | solution.py:778
  37.7 32.2 %collective-permute-start.6 = (bf16[768,768]{1,0:T(8,128)(2,1)S(1)}, bf16[768,768]{1,0:T(8,128)(2,1)S(1)}, u32[]{:S(2)}, u32[]{:S(2)}) collective-permute-start(bf16[768,768]{1,0:T(8,128)(2,1)S(1)} %copy-done.15), channel_id=1, source_target_pairs={{0,8},{8,0},{16,24},{24,16},{1,9},{9,1},{17,25},{25,17},{2,10},{10... | collective-permute-start | bytes 3538952 | tf_op jit(solution)/shard_map/ppermute | solution.py:778
  69.5 2.9 collective-permute-start.7
  73.5 37.3 %copy-start.14 = (bf16[768,768]{1,0:T(8,128)(2,1)S(1)}, bf16[768,768]{1,0:T(8,128)(2,1)}, u32[]{:S(2)}) copy-start(bf16[768,768]{1,0:T(8,128)(2,1)} %get-tuple-element.280.a0) | copy-start | bytes 3538948
  110.4 31.7 %collective-permute-start.9 = (bf16[2,768,768]{2,1,0:T(8,128)(2,1)}, bf16[2,768,768]{2,1,0:T(8,128)(2,1)S(1)}, u32[]{:S(2)}, u32[]{:S(2)}) collective-permute-start(bf16[2,768,768]{2,1,0:T(8,128)(2,1)} %get-tuple-element.273), channel_id=1, source_target_pairs={{0,8},{8,0},{16,24},{24,16},{1,9},{9,1},{17,25},{25,17},{2,10},{10... | collective-permute-start | bytes 7077896 | tf_op jit(solution)/shard_map/ppermute | solution.py:778
  110.7 28.1 %collective-permute-start.8 = (bf16[768,768]{1,0:T(8,128)(2,1)S(1)}, bf16[768,768]{1,0:T(8,128)(2,1)S(1)}, u32[]{:S(2)}, u32[]{:S(2)}) collective-permute-start(bf16[768,768]{1,0:T(8,128)(2,1)S(1)} %copy-done.14), channel_id=1, source_target_pairs={{0,16},{8,24},{16,0},{24,8},{1,17},{9,25},{17,1},{25,9},{2,18},{10... | collective-permute-start | bytes 3538952 | tf_op jit(solution)/shard_map/ppermute | solution.py:778
  112.1 31.5 %collective-permute-start.10 = (bf16[768,768]{1,0:T(8,128)(2,1)S(1)}, bf16[768,768]{1,0:T(8,128)(2,1)S(1)}, u32[]{:S(2)}, u32[]{:S(2)}) collective-permute-start(bf16[768,768]{1,0:T(8,128)(2,1)S(1)} %copy-done.14), channel_id=1, source_target_pairs={{0,8},{8,0},{16,24},{24,16},{1,9},{9,1},{17,25},{25,17},{2,10},{10... | collective-permute-start | bytes 3538952 | tf_op jit(solution)/shard_map/ppermute | solution.py:778
  138.8 4.8 %collective-permute-start.11 = (bf16[768,768]{1,0:T(8,128)(2,1)S(1)}, bf16[768,768]{1,0:T(8,128)(2,1)S(1)}, u32[]{:S(2)}, u32[]{:S(2)}) collective-permute-start(bf16[768,768]{1,0:T(8,128)(2,1)S(1)} %collective-permute-done.8.a2), channel_id=1, source_target_pairs={{0,8},{8,0},{16,24},{24,16},{1,9},{9,1},{17,25},{25,17},{2,10},{10... | collective-permute-start | bytes 3538952 | tf_op jit(solution)/shard_map/ppermute | solution.py:778
  182.6 32.2 %collective-permute-start.13 = (bf16[2,768,768]{2,1,0:T(8,128)(2,1)}, bf16[2,768,768]{2,1,0:T(8,128)(2,1)}, u32[]{:S(2)}, u32[]{:S(2)}) collective-permute-start(bf16[2,768,768]{2,1,0:T(8,128)(2,1)} %get-tuple-element.294), channel_id=1, source_target_pairs={{0,8},{8,0},{16,24},{24,16},{1,9},{9,1},{17,25},{25,17},{2,10},{10... | collective-permute-start | bytes 7077896 | tf_op jit(solution)/shard_map/ppermute | solution.py:778
  182.7 28.3 %collective-permute-start.12 = (bf16[768,768]{1,0:T(8,128)(2,1)S(1)}, bf16[768,768]{1,0:T(8,128)(2,1)S(1)}, u32[]{:S(2)}, u32[]{:S(2)}) collective-permute-start(bf16[768,768]{1,0:T(8,128)(2,1)S(1)} %add_convert_fusion.1), channel_id=1, source_target_pairs={{0,16},{8,24},{16,0},{24,8},{1,17},{9,25},{17,1},{25,9},{2,18},{10... | collective-permute-start | bytes 3538952 | tf_op jit(solution)/shard_map/ppermute | solution.py:778
  184.2 27.9 %copy-start.1 = (bf16[768,768]{1,0:T(8,128)(2,1)S(1)}, bf16[768,768]{1,0:T(8,128)(2,1)}, u32[]{:S(2)}) copy-start(bf16[768,768]{1,0:T(8,128)(2,1)} %get-tuple-element.290) | copy-start | bytes 3538948
  184.2 27.9 %copy-start.2 = (bf16[768,768]{1,0:T(8,128)(2,1)S(1)}, bf16[768,768]{1,0:T(8,128)(2,1)}, u32[]{:S(2)}) copy-start(bf16[768,768]{1,0:T(8,128)(2,1)} %get-tuple-element.291) | copy-start | bytes 3538948
  218.9 41.3 %collective-permute-start.15 = (bf16[768,768]{1,0:T(8,128)(2,1)}, bf16[768,768]{1,0:T(8,128)(2,1)}, u32[]{:S(2)}, u32[]{:S(2)}) collective-permute-start(bf16[768,768]{1,0:T(8,128)(2,1)} %add_convert_fusion), channel_id=1, source_target_pairs={{0,16},{8,24},{16,0},{24,8},{1,17},{9,25},{17,1},{25,9},{2,18},{10... | collective-permute-start | bytes 3538952 | tf_op jit(solution)/shard_map/ppermute | solution.py:778
  220.4 32.2 %collective-permute-start.14 = (bf16[384,768]{1,0:T(8,128)(2,1)}, bf16[384,768]{1,0:T(8,128)(2,1)}, u32[]{:S(2)}, u32[]{:S(2)}) collective-permute-start(bf16[384,768]{1,0:T(8,128)(2,1)} %fusion), channel_id=1, source_target_pairs={{0,1},{1,0},{2,3},{3,2},{4,5},{5,4},{6,7},{7,6},{8,9},{9,8},{10,11... | collective-permute-start | bytes 1769480 | tf_op jit(solution)/shard_map/ppermute | solution.py:778
  252.6 10.9 %collective-permute-start.16 = (bf16[2,384,768]{2,1,0:T(8,128)(2,1)}, bf16[2,384,768]{2,1,0:T(8,128)(2,1)S(1)}, u32[]{:S(2)}, u32[]{:S(2)}) collective-permute-start(bf16[2,384,768]{2,1,0:T(8,128)(2,1)} %get-tuple-element.320), channel_id=1, source_target_pairs={{0,8},{8,0},{16,24},{24,16},{1,9},{9,1},{17,25},{25,17},{2,10},{10... | collective-permute-start | bytes 3538952 | tf_op jit(solution)/shard_map/ppermute | solution.py:778
  253.8 6.4 %copy-start = (bf16[768,768]{1,0:T(8,128)(2,1)S(1)}, bf16[768,768]{1,0:T(8,128)(2,1)}, u32[]{:S(2)}) copy-start(bf16[768,768]{1,0:T(8,128)(2,1)} %get-tuple-element.317) | copy-start | bytes 3538948
  254.7 32.8 %collective-permute-start.17 = (bf16[96,768]{1,0:T(8,128)(2,1)}, bf16[96,768]{1,0:T(8,128)(2,1)S(1)}, u32[]{:S(2)}, u32[]{:S(2)}) collective-permute-start(bf16[96,768]{1,0:T(8,128)(2,1)} %get-tuple-element.481), channel_id=1, source_target_pairs={{0,2},{1,3},{2,4},{3,5},{4,6},{5,7},{6,0},{7,1},{8,10},{9,11},{10,... | collective-permute-start | bytes 442376 | tf_op jit(solution)/shard_map/ppermute | solution.py:783
  256.2 31.2 %collective-permute-start.18 = (bf16[96,768]{1,0:T(8,128)(2,1)}, bf16[96,768]{1,0:T(8,128)(2,1)S(1)}, u32[]{:S(2)}, u32[]{:S(2)}) collective-permute-start(bf16[96,768]{1,0:T(8,128)(2,1)} %get-tuple-element.480), channel_id=1, source_target_pairs={{0,4},{1,5},{2,6},{3,7},{4,0},{5,1},{6,2},{7,3},{8,12},{9,13},{10,... | collective-permute-start | bytes 442376 | tf_op jit(solution)/shard_map/ppermute | solution.py:783
  258.8 28.6 %collective-permute-start.19 = (bf16[96,768]{1,0:T(8,128)(2,1)}, bf16[96,768]{1,0:T(8,128)(2,1)}, u32[]{:S(2)}, u32[]{:S(2)}) collective-permute-start(bf16[96,768]{1,0:T(8,128)(2,1)} %get-tuple-element.479), channel_id=1, source_target_pairs={{0,6},{1,7},{2,0},{3,1},{4,2},{5,3},{6,4},{7,5},{8,14},{9,15},{10,... | collective-permute-start | bytes 442376 | tf_op jit(solution)/shard_map/ppermute | solution.py:783
  263.0 26.9 %collective-permute-start.20 = (bf16[384,768]{1,0:T(8,128)(2,1)}, bf16[384,768]{1,0:T(8,128)(2,1)}, u32[]{:S(2)}, u32[]{:S(2)}) collective-permute-start(bf16[384,768]{1,0:T(8,128)(2,1)} %get-tuple-element.492), channel_id=1, source_target_pairs={{0,1},{1,0},{2,3},{3,2},{4,5},{5,4},{6,7},{7,6},{8,9},{9,8},{10,11... | collective-permute-start | bytes 1769480 | tf_op jit(solution)/shard_map/ppermute | solution.py:778
  263.8 31.0 %collective-permute-start.22 = (bf16[384,768]{1,0:T(8,128)(2,1)S(1)}, bf16[384,768]{1,0:T(8,128)(2,1)}, u32[]{:S(2)}, u32[]{:S(2)}) collective-permute-start(bf16[384,768]{1,0:T(8,128)(2,1)S(1)} %add_convert_fusion.3), channel_id=1, source_target_pairs={{0,16},{8,24},{16,0},{24,8},{1,17},{9,25},{17,1},{25,9},{2,18},{10... | collective-permute-start | bytes 1769480 | tf_op jit(solution)/shard_map/ppermute | solution.py:778
  287.5 6.5 %collective-permute-start.21 = (bf16[2,384,768]{2,1,0:T(8,128)(2,1)}, bf16[2,384,768]{2,1,0:T(8,128)(2,1)S(1)}, u32[]{:S(2)}, u32[]{:S(2)}) collective-permute-start(bf16[2,384,768]{2,1,0:T(8,128)(2,1)} %get-tuple-element.340), channel_id=1, source_target_pairs={{0,8},{8,0},{16,24},{24,16},{1,9},{9,1},{17,25},{25,17},{2,10},{10... | collective-permute-start | bytes 3538952 | tf_op jit(solution)/shard_map/ppermute | solution.py:778
  288.5 24.1 %collective-permute-start.23 = (bf16[96,768]{1,0:T(8,128)(2,1)S(1)}, bf16[96,768]{1,0:T(8,128)(2,1)}, u32[]{:S(2)}, u32[]{:S(2)}) collective-permute-start(bf16[96,768]{1,0:T(8,128)(2,1)S(1)} %add_convert_fusion.5), channel_id=1, source_target_pairs={{0,2},{1,3},{2,4},{3,5},{4,6},{5,7},{6,0},{7,1},{8,10},{9,11},{10,... | collective-permute-start | bytes 442376 | tf_op jit(solution)/shard_map/ppermute | solution.py:783
  289.3 26.3 %collective-permute-start.24 = (bf16[96,768]{1,0:T(8,128)(2,1)S(1)}, bf16[96,768]{1,0:T(8,128)(2,1)}, u32[]{:S(2)}, u32[]{:S(2)}) collective-permute-start(bf16[96,768]{1,0:T(8,128)(2,1)S(1)} %add_convert_fusion.5), channel_id=1, source_target_pairs={{0,4},{1,5},{2,6},{3,7},{4,0},{5,1},{6,2},{7,3},{8,12},{9,13},{10,... | collective-permute-start | bytes 442376 | tf_op jit(solution)/shard_map/ppermute | solution.py:783
  289.9 27.1 %collective-permute-start.25 = (bf16[96,768]{1,0:T(8,128)(2,1)S(1)}, bf16[96,768]{1,0:T(8,128)(2,1)S(1)}, u32[]{:S(2)}, u32[]{:S(2)}) collective-permute-start(bf16[96,768]{1,0:T(8,128)(2,1)S(1)} %add_convert_fusion.5), channel_id=1, source_target_pairs={{0,6},{1,7},{2,0},{3,1},{4,2},{5,3},{6,4},{7,5},{8,14},{9,15},{10,... | collective-permute-start | bytes 442376 | tf_op jit(solution)/shard_map/ppermute | solution.py:783
  293.9 25.1 %collective-permute-start.26 = (bf16[96,768]{1,0:T(8,128)(2,1)S(1)}, bf16[96,768]{1,0:T(8,128)(2,1)S(1)}, u32[]{:S(2)}, u32[]{:S(2)}) collective-permute-start(bf16[96,768]{1,0:T(8,128)(2,1)S(1)} %get-tuple-element.474), channel_id=1, source_target_pairs={{0,2},{1,3},{2,4},{3,5},{4,6},{5,7},{6,0},{7,1},{8,10},{9,11},{10,... | collective-permute-start | bytes 442376 | tf_op jit(solution)/shard_map/ppermute | solution.py:783
  294.8 25.7 %collective-permute-start.27 = (bf16[96,768]{1,0:T(8,128)(2,1)S(1)}, bf16[96,768]{1,0:T(8,128)(2,1)S(1)}, u32[]{:S(2)}, u32[]{:S(2)}) collective-permute-start(bf16[96,768]{1,0:T(8,128)(2,1)S(1)} %get-tuple-element.473), channel_id=1, source_target_pairs={{0,4},{1,5},{2,6},{3,7},{4,0},{5,1},{6,2},{7,3},{8,12},{9,13},{10,... | collective-permute-start | bytes 442376 | tf_op jit(solution)/shard_map/ppermute | solution.py:783
  312.6 7.9 %collective-permute-start.28 = (bf16[96,768]{1,0:T(8,128)(2,1)S(1)}, bf16[96,768]{1,0:T(8,128)(2,1)S(1)}, u32[]{:S(2)}, u32[]{:S(2)}) collective-permute-start(bf16[96,768]{1,0:T(8,128)(2,1)S(1)} %get-tuple-element.472), channel_id=1, source_target_pairs={{0,6},{1,7},{2,0},{3,1},{4,2},{5,3},{6,4},{7,5},{8,14},{9,15},{10,... | collective-permute-start | bytes 442376 | tf_op jit(solution)/shard_map/ppermute | solution.py:783
  315.5 7.7 %collective-permute-start.29 = (bf16[192,768]{1,0:T(8,128)(2,1)S(1)}, bf16[192,768]{1,0:T(8,128)(2,1)S(1)}, u32[]{:S(2)}, u32[]{:S(2)}) collective-permute-start(bf16[192,768]{1,0:T(8,128)(2,1)S(1)} %fusion.2), channel_id=1, source_target_pairs={{0,1},{1,0},{2,3},{3,2},{4,5},{5,4},{6,7},{7,6},{8,9},{9,8},{10,11... | collective-permute-start | bytes 884744 | tf_op jit(solution)/shard_map/ppermute | solution.py:778
  317.0 7.6 %collective-permute-start.30 = (f32[144,128]{1,0:T(8,128)}, f32[144,128]{1,0:T(8,128)S(1)}, u32[]{:S(2)}, u32[]{:S(2)}) collective-permute-start(f32[144,128]{1,0:T(8,128)} %shard_map.142), channel_id=1, source_target_pairs={{0,8},{8,0},{16,24},{24,16},{1,9},{9,1},{17,25},{25,17},{2,10},{10... | collective-permute-start | bytes 221192 | tf_op jit(solution)/shard_map/ppermute | solution.py:778
  319.0 15.8 %collective-permute-start.31 = (bf16[384,768]{1,0:T(8,128)(2,1)S(1)}, bf16[384,768]{1,0:T(8,128)(2,1)S(1)}, u32[]{:S(2)}, u32[]{:S(2)}) collective-permute-start(bf16[384,768]{1,0:T(8,128)(2,1)S(1)} %add_convert_fusion.2), channel_id=1, source_target_pairs={{0,16},{8,24},{16,0},{24,8},{1,17},{9,25},{17,1},{25,9},{2,18},{10... | collective-permute-start | bytes 1769480 | tf_op jit(solution)/shard_map/ppermute | solution.py:778
  320.5 18.6 %collective-permute-start.33 = (bf16[96,768]{1,0:T(8,128)(2,1)S(1)}, bf16[96,768]{1,0:T(8,128)(2,1)S(1)}, u32[]{:S(2)}, u32[]{:S(2)}) collective-permute-start(bf16[96,768]{1,0:T(8,128)(2,1)S(1)} %add_convert_fusion.4), channel_id=1, source_target_pairs={{0,2},{1,3},{2,4},{3,5},{4,6},{5,7},{6,0},{7,1},{8,10},{9,11},{10,... | collective-permute-start | bytes 442376 | tf_op jit(solution)/shard_map/ppermute | solution.py:783
  320.6 19.5 %collective-permute-start.34 = (bf16[96,768]{1,0:T(8,128)(2,1)S(1)}, bf16[96,768]{1,0:T(8,128)(2,1)S(1)}, u32[]{:S(2)}, u32[]{:S(2)}) collective-permute-start(bf16[96,768]{1,0:T(8,128)(2,1)S(1)} %add_convert_fusion.4), channel_id=1, source_target_pairs={{0,4},{1,5},{2,6},{3,7},{4,0},{5,1},{6,2},{7,3},{8,12},{9,13},{10,... | collective-permute-start | bytes 442376 | tf_op jit(solution)/shard_map/ppermute | solution.py:783
  323.3 19.9 %collective-permute-start.35 = (bf16[96,768]{1,0:T(8,128)(2,1)S(1)}, bf16[96,768]{1,0:T(8,128)(2,1)S(1)}, u32[]{:S(2)}, u32[]{:S(2)}) collective-permute-start(bf16[96,768]{1,0:T(8,128)(2,1)S(1)} %add_convert_fusion.4), channel_id=1, source_target_pairs={{0,6},{1,7},{2,0},{3,1},{4,2},{5,3},{6,4},{7,5},{8,14},{9,15},{10,... | collective-permute-start | bytes 442376 | tf_op jit(solution)/shard_map/ppermute | solution.py:783
  324.6 27.9 %collective-permute-start.41 = (bf16[384,768]{1,0:T(8,128)(2,1)S(1)}, bf16[384,768]{1,0:T(8,128)(2,1)S(1)}, u32[]{:S(2)}, u32[]{:S(2)}) collective-permute-start(bf16[384,768]{1,0:T(8,128)(2,1)S(1)} %bitcast.144), channel_id=1, source_target_pairs={{0,1},{1,0},{2,3},{3,2},{4,5},{5,4},{6,7},{7,6},{8,9},{9,8},{10,11... | collective-permute-start | bytes 1769480 | tf_op jit(solution)/shard_map/ppermute | solution.py:778
  334.8 4.4 %collective-permute-start.32 = (f32[144,128]{1,0:T(8,128)S(1)}, f32[144,128]{1,0:T(8,128)S(1)}, u32[]{:S(2)}, u32[]{:S(2)}) collective-permute-start(f32[144,128]{1,0:T(8,128)S(1)} %add.291), channel_id=1, source_target_pairs={{0,16},{8,24},{16,0},{24,8},{1,17},{9,25},{17,1},{25,9},{2,18},{10... | collective-permute-start | bytes 221192 | tf_op jit(solution)/shard_map/ppermute | solution.py:778
  339.1 6.6 %collective-permute-start.36 = (bf16[48,768]{1,0:T(8,128)(2,1)S(1)}, bf16[48,768]{1,0:T(8,128)(2,1)S(1)}, u32[]{:S(2)}, u32[]{:S(2)}) collective-permute-start(bf16[48,768]{1,0:T(8,128)(2,1)S(1)} %get-tuple-element.491), channel_id=1, source_target_pairs={{0,2},{1,3},{2,4},{3,5},{4,6},{5,7},{6,0},{7,1},{8,10},{9,11},{10,... | collective-permute-start | bytes 221192 | tf_op jit(solution)/shard_map/ppermute | solution.py:783
  339.2 8.0 %collective-permute-start.37 = (bf16[48,768]{1,0:T(8,128)(2,1)S(1)}, bf16[48,768]{1,0:T(8,128)(2,1)S(1)}, u32[]{:S(2)}, u32[]{:S(2)}) collective-permute-start(bf16[48,768]{1,0:T(8,128)(2,1)S(1)} %get-tuple-element.490), channel_id=1, source_target_pairs={{0,4},{1,5},{2,6},{3,7},{4,0},{5,1},{6,2},{7,3},{8,12},{9,13},{10,... | collective-permute-start | bytes 221192 | tf_op jit(solution)/shard_map/ppermute | solution.py:783
  340.1 7.0 %collective-permute-start.38 = (bf16[48,768]{1,0:T(8,128)(2,1)S(1)}, bf16[48,768]{1,0:T(8,128)(2,1)S(1)}, u32[]{:S(2)}, u32[]{:S(2)}) collective-permute-start(bf16[48,768]{1,0:T(8,128)(2,1)S(1)} %get-tuple-element.489), channel_id=1, source_target_pairs={{0,6},{1,7},{2,0},{3,1},{4,2},{5,3},{6,4},{7,5},{8,14},{9,15},{10,... | collective-permute-start | bytes 221192 | tf_op jit(solution)/shard_map/ppermute | solution.py:783
  343.1 8.0 %collective-permute-start.39 = (bf16[192,768]{1,0:T(8,128)(2,1)S(1)}, bf16[192,768]{1,0:T(8,128)(2,1)S(1)}, u32[]{:S(2)}, u32[]{:S(2)}) collective-permute-start(bf16[192,768]{1,0:T(8,128)(2,1)S(1)} %fusion.3), channel_id=1, source_target_pairs={{0,1},{1,0},{2,3},{3,2},{4,5},{5,4},{6,7},{7,6},{8,9},{9,8},{10,11... | collective-permute-start | bytes 884744 | tf_op jit(solution)/shard_map/ppermute | solution.py:778
  345.7 6.2 %collective-permute-start.40 = (f32[144,128]{1,0:T(8,128)S(1)}, f32[144,128]{1,0:T(8,128)S(1)}, u32[]{:S(2)}, u32[]{:S(2)}) collective-permute-start(f32[144,128]{1,0:T(8,128)S(1)} %add.294), channel_id=1, source_target_pairs={{0,1},{1,0},{2,3},{3,2},{4,5},{5,4},{6,7},{7,6},{8,9},{9,8},{10,11... | collective-permute-start | bytes 221192 | tf_op jit(solution)/shard_map/ppermute | solution.py:778
  347.2 17.1 %collective-permute-start.44 = (bf16[48,768]{1,0:T(8,128)(2,1)S(1)}, bf16[48,768]{1,0:T(8,128)(2,1)S(1)}, u32[]{:S(2)}, u32[]{:S(2)}) collective-permute-start(bf16[48,768]{1,0:T(8,128)(2,1)S(1)} %add_convert_fusion.7), channel_id=1, source_target_pairs={{0,2},{1,3},{2,4},{3,5},{4,6},{5,7},{6,0},{7,1},{8,10},{9,11},{10,... | collective-permute-start | bytes 221192 | tf_op jit(solution)/shard_map/ppermute | solution.py:783
  348.6 18.8 %collective-permute-start.45 = (bf16[48,768]{1,0:T(8,128)(2,1)S(1)}, bf16[48,768]{1,0:T(8,128)(2,1)S(1)}, u32[]{:S(2)}, u32[]{:S(2)}) collective-permute-start(bf16[48,768]{1,0:T(8,128)(2,1)S(1)} %add_convert_fusion.7), channel_id=1, source_target_pairs={{0,4},{1,5},{2,6},{3,7},{4,0},{5,1},{6,2},{7,3},{8,12},{9,13},{10,... | collective-permute-start | bytes 221192 | tf_op jit(solution)/shard_map/ppermute | solution.py:783
  351.2 17.1 %collective-permute-start.46 = (bf16[48,768]{1,0:T(8,128)(2,1)S(1)}, bf16[48,768]{1,0:T(8,128)(2,1)S(1)}, u32[]{:S(2)}, u32[]{:S(2)}) collective-permute-start(bf16[48,768]{1,0:T(8,128)(2,1)S(1)} %add_convert_fusion.7), channel_id=1, source_target_pairs={{0,6},{1,7},{2,0},{3,1},{4,2},{5,3},{6,4},{7,5},{8,14},{9,15},{10,... | collective-permute-start | bytes 221192 | tf_op jit(solution)/shard_map/ppermute | solution.py:783
  351.9 25.3 %collective-permute-start.50 = (bf16[384,768]{1,0:T(8,128)(2,1)S(1)}, bf16[384,768]{1,0:T(8,128)(2,1)S(1)}, u32[]{:S(2)}, u32[]{:S(2)}) collective-permute-start(bf16[384,768]{1,0:T(8,128)(2,1)S(1)} %bitcast.146), channel_id=1, source_target_pairs={{0,1},{1,0},{2,3},{3,2},{4,5},{5,4},{6,7},{7,6},{8,9},{9,8},{10,11... | collective-permute-start | bytes 1769480 | tf_op jit(solution)/shard_map/ppermute | solution.py:778
  352.5 4.4 %collective-permute-start.42 = (f32[144,128]{1,0:T(8,128)S(1)}, f32[144,128]{1,0:T(8,128)S(1)}, u32[]{:S(2)}, u32[]{:S(2)}) collective-permute-start(f32[144,128]{1,0:T(8,128)S(1)} %add.299), channel_id=1, source_target_pairs={{0,2},{1,3},{2,0},{3,1},{4,6},{5,7},{6,4},{7,5},{8,10},{9,11},{10,... | collective-permute-start | bytes 221192 | tf_op jit(solution)/shard_map/ppermute | solution.py:778
  356.9 5.3 %collective-permute-start.43 = (f32[144,128]{1,0:T(8,128)S(1)}, f32[144,128]{1,0:T(8,128)S(1)}, u32[]{:S(2)}, u32[]{:S(2)}) collective-permute-start(f32[144,128]{1,0:T(8,128)S(1)} %add.300), channel_id=1, source_target_pairs={{0,4},{1,5},{2,6},{3,7},{4,0},{5,1},{6,2},{7,3},{8,12},{9,13},{10,... | collective-permute-start | bytes 221192 | tf_op jit(solution)/shard_map/ppermute | solution.py:778
  362.3 8.0 %collective-permute-start.47 = (bf16[48,768]{1,0:T(8,128)(2,1)S(1)}, bf16[48,768]{1,0:T(8,128)(2,1)S(1)}, u32[]{:S(2)}, u32[]{:S(2)}) collective-permute-start(bf16[48,768]{1,0:T(8,128)(2,1)S(1)} %get-tuple-element.488), channel_id=1, source_target_pairs={{0,2},{1,3},{2,4},{3,5},{4,6},{5,7},{6,0},{7,1},{8,10},{9,11},{10,... | collective-permute-start | bytes 221192 | tf_op jit(solution)/shard_map/ppermute | solution.py:783
  364.3 5.9 %collective-permute-start.48 = (bf16[48,768]{1,0:T(8,128)(2,1)S(1)}, bf16[48,768]{1,0:T(8,128)(2,1)S(1)}, u32[]{:S(2)}, u32[]{:S(2)}) collective-permute-start(bf16[48,768]{1,0:T(8,128)(2,1)S(1)} %get-tuple-element.487), channel_id=1, source_target_pairs={{0,4},{1,5},{2,6},{3,7},{4,0},{5,1},{6,2},{7,3},{8,12},{9,13},{10,... | collective-permute-start | bytes 221192 | tf_op jit(solution)/shard_map/ppermute | solution.py:783
  367.4 6.0 %collective-permute-start.49 = (bf16[48,768]{1,0:T(8,128)(2,1)S(1)}, bf16[48,768]{1,0:T(8,128)(2,1)S(1)}, u32[]{:S(2)}, u32[]{:S(2)}) collective-permute-start(bf16[48,768]{1,0:T(8,128)(2,1)S(1)} %get-tuple-element.486), channel_id=1, source_target_pairs={{0,6},{1,7},{2,0},{3,1},{4,2},{5,3},{6,4},{7,5},{8,14},{9,15},{10,... | collective-permute-start | bytes 221192 | tf_op jit(solution)/shard_map/ppermute | solution.py:783
  368.3 10.1 %collective-permute-start.51 = (bf16[192,768]{1,0:T(8,128)(2,1)S(1)}, bf16[192,768]{1,0:T(8,128)(2,1)S(1)}, u32[]{:S(2)}, u32[]{:S(2)}) collective-permute-start(bf16[192,768]{1,0:T(8,128)(2,1)S(1)} %bitcast.154), channel_id=1, source_target_pairs={{0,1},{1,0},{2,3},{3,2},{4,5},{5,4},{6,7},{7,6},{8,9},{9,8},{10,11... | collective-permute-start | bytes 884744 | tf_op jit(solution)/shard_map/ppermute | solution.py:778
  373.4 6.3 %collective-permute-start.52 = (bf16[48,768]{1,0:T(8,128)(2,1)S(1)}, bf16[48,768]{1,0:T(8,128)(2,1)S(1)}, u32[]{:S(2)}, u32[]{:S(2)}) collective-permute-start(bf16[48,768]{1,0:T(8,128)(2,1)S(1)} %add_convert_fusion.6), channel_id=1, source_target_pairs={{0,2},{1,3},{2,4},{3,5},{4,6},{5,7},{6,0},{7,1},{8,10},{9,11},{10,... | collective-permute-start | bytes 221192 | tf_op jit(solution)/shard_map/ppermute | solution.py:783
  374.0 6.8 %collective-permute-start.53 = (bf16[48,768]{1,0:T(8,128)(2,1)S(1)}, bf16[48,768]{1,0:T(8,128)(2,1)S(1)}, u32[]{:S(2)}, u32[]{:S(2)}) collective-permute-start(bf16[48,768]{1,0:T(8,128)(2,1)S(1)} %add_convert_fusion.6), channel_id=1, source_target_pairs={{0,4},{1,5},{2,6},{3,7},{4,0},{5,1},{6,2},{7,3},{8,12},{9,13},{10,... | collective-permute-start | bytes 221192 | tf_op jit(solution)/shard_map/ppermute | solution.py:783
  375.9 5.0 %collective-permute-start.54 = (bf16[48,768]{1,0:T(8,128)(2,1)S(1)}, bf16[48,768]{1,0:T(8,128)(2,1)S(1)}, u32[]{:S(2)}, u32[]{:S(2)}) collective-permute-start(bf16[48,768]{1,0:T(8,128)(2,1)S(1)} %add_convert_fusion.6), channel_id=1, source_target_pairs={{0,6},{1,7},{2,0},{3,1},{4,2},{5,3},{6,4},{7,5},{8,14},{9,15},{10,... | collective-permute-start | bytes 221192 | tf_op jit(solution)/shard_map/ppermute | solution.py:783
  378.5 5.7 %copy-start.3 = (bf16[8,197,768]{2,1,0:T(8,128)(2,1)S(1)}, bf16[8,197,768]{2,1,0:T(8,128)(2,1)}, u32[]{:S(2)}) copy-start(bf16[8,197,768]{2,1,0:T(8,128)(2,1)} %get-tuple-element.448) | copy-start | bytes 7262212
  380.9 23.4 %collective-permute-start.55 = (bf16[192,768]{1,0:T(8,128)(2,1)S(1)}, bf16[192,768]{1,0:T(8,128)(2,1)S(1)}, u32[]{:S(2)}, u32[]{:S(2)}) collective-permute-start(bf16[192,768]{1,0:T(8,128)(2,1)S(1)} %bitcast.152), channel_id=1, source_target_pairs={{0,1},{1,0},{2,3},{3,2},{4,5},{5,4},{6,7},{7,6},{8,9},{9,8},{10,11... | collective-permute-start | bytes 884744 | tf_op jit(solution)/shard_map/ppermute | solution.py:778
  (16 other events, 31.3 us)
where the time goes:
time: 420 us; the launch traced here: 414 us
  Pallas kernels  205 us (49%)
  waiting for transfers between devices  96 us (23%)
  starting transfers between devices  63.4 us (15%)
  local copies, waits for them, and re-layouts  30.5 us (7%)
  other arithmetic  16.6 us (4%)
    ppermute x32, waiting for transfers between devices, swap(): return lax.ppermute(value, axis, pairs)  88.6 us
    pallas_call x2, Pallas kernels, call_feed(): pl.pallas_call(functools.partial(feed, seq, part, tall), grid=(ROW_STEPS...  73.8 us
    pallas_call x2, Pallas kernels, call_attn_backward(): pl.pallas_call(functools.partial(attn_backward, seq, images, group), grid...  53.6 us
    ppermute x24, starting transfers between devices, turn(): lax.ppermute(value, axis, [(i, (i + unit * distance) % size) for i in ran...  34.7 us
    pallas_call x1, Pallas kernels, call_attn_forward(): pl.pallas_call(functools.partial(attn_forward, seq), grid=(images,), in_s...  29.6 us
    ppermute x32, starting transfers between devices, swap(): return lax.ppermute(value, axis, pairs)  28.7 us
    pallas_call x2, Pallas kernels, adam(): pl.pallas_call(functools.partial(adam_kernel, block, count, scale, len(bo...  24.1 us
    pallas_call x1, Pallas kernels, call_input_backward(): pl.pallas_call(functools.partial(input_backward, seq), grid=(images // st...  13.3 us
  transfers between devices with their start and end apart: 56, of which 17 were waited for; matrix products, arithmetic and copies ran while one was open for 8% of the time, Pallas kernels for 29%

commit v1 on v0

--- a/solution.py
+++ b/solution.py
@@ -357,6 +357,20 @@
     )(x, shard, extra, *boxes)
 
 
+def hand_out(index, box, outs, sems):
+    copies = [pltpu.make_async_copy(box.at[k], out, sems.at[k]) for k, out in enumerate(outs)]
+    for k, copy in enumerate(copies):
+
+        @pl.when(index == k)
+        def _(copy=copy):
+            copy.start()
+
+    @pl.when(index == len(outs) - 1)
+    def _():
+        for copy in copies:
+            copy.wait()
+
+
 HALF = FF // 2
 ROW_STEPS = 4
 
@@ -367,7 +381,7 @@
         before_ref, out_ref, gs_ref, *refs = refs
     else:
         out_ref, gs_ref, cot_sum, *refs = refs
-    sum_ref, edge_ref, other_ref, mine_ref, up_w, down_w, bias, second_all, cot_all, act_all, pre_all, box, sems = refs
+    sum_ref, edge_ref, *outs, up_w, down_w, bias, second_all, cot_all, act_all, pre_all, box, sems, box_sems = refs
     step = pl.program_id(0)
     shard = shard_ref[0]
 
@@ -419,7 +433,7 @@
         gs_ref[...] = grad_second
 
     index = step - ROW_STEPS
-    side = jnp.bitwise_xor(shard // 2, index % 2)
+    side = jnp.bitwise_xor(shard // 2, 1 - index % 2)
     core = jnp.where(index >= 2, shard % 2, 1 - shard % 2)
 
     @pl.when((index >= 0) & (side == 0))
@@ -427,7 +441,7 @@
         left = second_all[:, pl.ds(pl.multiple_of(384 * core, 128), 384)]
         for h in range(2):
             grad = dot_tn(left, pre_all[:, 768 * h : 768 * h + 768])
-            box[384 * h : 384 * h + 384, :] = grad.astype(BF)
+            box[index, 384 * h : 384 * h + 384, :] = grad.astype(BF)
 
             @pl.when(core == 0)
             def _(grad=grad, h=h):
@@ -437,19 +451,13 @@
     def _():
         left = act_all[:, pl.ds(pl.multiple_of(768 * core, 128), 768)]
         grad = dot_tn(left, cot_all[...])
-        box[...] = grad.astype(BF)
+        box[index] = grad.astype(BF)
 
         @pl.when(core == 0)
         def _():
             edge_ref[1:2, 0:768] = grad[767:768]
 
-    @pl.when((index >= 0) & (index < 2))
-    def _():
-        other_ref[0] = box[...]
-
-    @pl.when(index >= 2)
-    def _():
-        mine_ref[0] = box[...]
+    hand_out(index, box, outs, box_sems)
 
 
 def call_feed(seq, part, shard, extra, boxes, second, cot, result, before=None):
@@ -460,16 +468,15 @@
     row = lambda i: jnp.minimum(i, ROW_STEPS - 1)
     block = pl.BlockSpec((tall, D), lambda i: (row(i), 0))
     out = pl.BlockSpec((tall // T, seq, D), lambda i: (row(i), 0, 0)) if last else block
-    grads = lambda first: pl.BlockSpec((1, D, D), lambda i: (jnp.clip(i - ROW_STEPS - first, 0, 1), 0, 0))
     small = lambda width: pl.BlockSpec((8, width), lambda i: (0, 0))
     return pl.pallas_call(
         functools.partial(feed, seq, part, tall),
         grid=(ROW_STEPS + 4,),
         in_specs=[SMEM, whole(extra)] + [ANYWHERE] * 4 + [block] * (4 if last else 3),
-        out_specs=[out, block] + ([] if last else [small(D)]) + [small(HALF), small(HALF), grads(0), grads(2)],
+        out_specs=[out, block] + ([] if last else [small(D)]) + [small(HALF), small(HALF)] + [ANYWHERE] * 4,
         out_shape=[sds((images, seq, D), BF) if last else sds((rows, D), F32), sds((rows, D), F32)]
         + ([] if last else [sds((8, D), F32)])
-        + [sds((8, HALF), F32), sds((8, HALF), F32), sds((2, D, D), BF), sds((2, D, D), BF)],
+        + [sds((8, HALF), F32), sds((8, HALF), F32)] + [sds((D, D), BF)] * 4,
         scratch_shapes=[
             pltpu.VMEM((HALF, D), BF),
             pltpu.VMEM((HALF, D), BF),
@@ -478,8 +485,9 @@
             pltpu.VMEM((rows, D), BF),
             pltpu.VMEM((rows, HALF), BF),
             pltpu.VMEM((rows, HALF), BF),
-            pltpu.VMEM((D, D), BF),
+            pltpu.VMEM((4, D, D), BF),
             pltpu.SemaphoreType.DMA((4, 2)),
+            pltpu.SemaphoreType.DMA((4,)),
         ],
         compiler_params=params(60),
     )(shard, extra, *boxes, second, cot, result, *([before] if last else []))
@@ -488,27 +496,51 @@
 WIDE = 384
 
 
-def attn_backward(seq, images, group, shard_ref, log_ref, qkv_ref, first_ref, att_ref, *refs):
+def attn_backward(seq, group, base, count, last, shard_ref, log_ref, qkv_ref, first_ref, att_ref, *refs):
     step = pl.program_id(0)
     shard = shard_ref[0]
     if group == 0:
-        gs_ref, hid_ref, cot_ref, vec_ref, proj_w, grad_ref, head_sum, low_ref, ga_ref, gh_ref, sum_ref, *refs = refs
+        gs_ref, hid_ref, cot_ref, vec_ref, proj_w, *refs = refs
     else:
-        low_ref, ga_ref, grad_ref, head_sum, *refs = refs
-    edge_ref, other_ref, mine_ref, grad_all, first_all, low_all, att_all, box = refs
+        low_ref, ga_ref, *refs = refs
+    if last:
+        if group == 0:
+            head_before, sum_before, first_any, att_any, low_any, grad_any, _, _, *refs = refs
+        else:
+            head_before, first_any, att_any, low_any, grad_any, *refs = refs
+    grad_ref, head_sum, *refs = refs
+    if group == 0:
+        low_ref, ga_ref, gh_ref, sum_ref, *refs = refs
+    if last:
+        edge_ref, *outs, grad_all, first_all, low_all, att_all, box, box_sems, load_sems = refs
+        done = pl.ds(0, base * T)
+        loads = [
+            pltpu.make_async_copy(grad_any.at[done], grad_all.at[done], load_sems.at[0]),
+            pltpu.make_async_copy(first_any.at[done], first_all.at[done], load_sems.at[1]),
+            pltpu.make_async_copy(low_any.at[done], low_all.at[done], load_sems.at[2]),
+            pltpu.make_async_copy(
+                att_any.at[done, pl.ds(WIDE * group, WIDE)], att_all.at[done], load_sems.at[3]
+            ),
+        ]
 
     @pl.when(step == 0)
     def _():
-        head_sum[...] = jnp.zeros_like(head_sum)
-        edge_ref[...] = jnp.zeros_like(edge_ref)
+        if last:
+            for load in loads:
+                load.start()
+            edge_ref[...] = jnp.zeros_like(edge_ref)
+            head_sum[...] = head_before[...]
+        else:
+            head_sum[...] = jnp.zeros_like(head_sum)
         if group == 0:
-            sum_ref[...] = jnp.zeros_like(sum_ref)
-
-    @pl.when(step < images)
-    def _():
-        at_rows = pl.ds(pl.multiple_of(step * T, 16), T)
-        first_all[at_rows, :] = first_ref[...]
-        att_all[at_rows, :] = att_ref[...]
+            sum_ref[...] = sum_before[...] if last else jnp.zeros_like(sum_ref)
+
+    @pl.when(step < count)
+    def _():
+        at_rows = pl.ds(pl.multiple_of((step + base) * T, 16), T)
+        if last:
+            first_all[at_rows, :] = first_ref[...]
+            att_all[at_rows, :] = att_ref[...]
         if group == 0:
             gs = gs_ref[...]
             normed, spread = normed_of(hid_ref[...])
@@ -523,7 +555,8 @@
             gh_low = gh.astype(BF)
             low_ref[...] = gh_low
             ga_ref[...] = dot_nt(gh_low, proj_w[...]).astype(BF)
-        low_all[at_rows, :] = low_ref[...]
+        if last:
+            low_all[at_rows, :] = low_ref[...]
         low = lax.broadcasted_iota(jnp.int32, (T, LANES), 1) < 64
         real = lax.broadcasted_iota(jnp.int32, (2, T, T), 1) < seq
         eighth = jnp.asarray(0.125, BF)
@@ -556,16 +589,25 @@
                 cols = slice(WIDE * part + at, WIDE * part + at + LANES)
                 grad = grad.astype(BF)
                 grad_ref[:, cols] = grad
-                grad_all[at_rows, cols] = grad
-
-    index = step - images
-    side = jnp.bitwise_xor(shard // 2, index % 2)
+                if last:
+                    grad_all[at_rows, cols] = grad
+
+    if not last:
+        return
+
+    @pl.when(step == count)
+    def _():
+        for load in loads:
+            load.wait()
+
+    index = step - count
+    side = jnp.bitwise_xor(shard // 2, 1 - index % 2)
     core = jnp.where(index >= 2, shard % 2, 1 - shard % 2)
     share = 2 * side + core
 
     @pl.when((index >= 0) & (share == 3))
     def _():
-        box[...] = dot_tn(att_all[...], low_all[...]).astype(BF)
+        box[index] = dot_tn(att_all[...], low_all[...]).astype(BF)
 
     @pl.when((index >= 0) & (share != 3))
     def _():
@@ -573,7 +615,7 @@
         for part in range(3):
             cols = slice(WIDE * part, WIDE * part + WIDE)
             for u in range(2):
-                box[128 * part : 128 * part + 128, WIDE * u : WIDE * u + WIDE] = grad[
+                box[index, 128 * part : 128 * part + 128, WIDE * u : WIDE * u + WIDE] = grad[
                     128 * u : 128 * u + 128, cols
                 ].astype(BF)
 
@@ -585,22 +627,15 @@
         def _():
             edge_ref[1:2, :] = grad[0:1]
 
-    @pl.when((index >= 0) & (index < 2))
-    def _():
-        other_ref[0] = box[...]
-
-    @pl.when(index >= 2)
-    def _():
-        mine_ref[0] = box[...]
-
-
-def call_attn_backward(seq, group, shard, log_total, qkv, first, attended, *more):
+    hand_out(index, box, outs, box_sems)
+
+
+def call_attn_backward(seq, group, base, count, shard, log_total, qkv, first, attended, *more, before=()):
     rows = first.shape[0]
-    images = rows // T
-    row = lambda i: jnp.minimum(i, images - 1)
+    last = len(before) > 0
+    row = lambda i: jnp.minimum(i, count - 1) + base
     block = lambda width, col=0: pl.BlockSpec((T, width), lambda i: (row(i), col))
     small = lambda width: pl.BlockSpec((8, width), lambda i: (0, 0))
-    grads = lambda at: pl.BlockSpec((1, WIDE, D), lambda i: (jnp.clip(i - images - at, 0, 1), 0, 0))
     in_specs = [SMEM, pl.BlockSpec((1, HEADS, T), lambda i: (row(i), 0, 0)), block(2304), block(D), block(WIDE, group)]
     out_specs = [block(3 * WIDE), small(WIDE)]
     out_shape = [sds((rows, 3 * WIDE), BF), sds((8, WIDE), F32)]
@@ -610,21 +645,40 @@
         out_shape += [sds((rows, D), BF), sds((rows, D), BF), sds((rows, D), F32), sds((8, D), F32)]
     else:
         in_specs += [block(D), block(WIDE, 1)]
-    return pl.pallas_call(
-        functools.partial(attn_backward, seq, images, group),
-        grid=(images + 4,),
-        in_specs=in_specs,
-        out_specs=out_specs + [small(3 * WIDE), grads(0), grads(2)],
-        out_shape=out_shape + [sds((8, 3 * WIDE), F32), sds((2, WIDE, D), BF), sds((2, WIDE, D), BF)],
-        scratch_shapes=[
+    aliases, scratch, extra = {}, [], []
+    if last:
+        at = len(in_specs)
+        if group == 0:
+            grad, head, low, ga, gh, total = before
+            extra = [head, total, first, attended, low, grad, ga, gh]
+            in_specs += [whole(head), whole(total)] + [ANYWHERE] * 6
+            aliases = {at + 4: 2, at + 5: 0, at + 6: 3, at + 7: 4}
+        else:
+            grad, head = before
+            extra = [head, first, attended, more[0], grad]
+            in_specs += [whole(head)] + [ANYWHERE] * 4
+            aliases = {at + 4: 0}
+        out_specs += [small(3 * WIDE)] + [ANYWHERE] * 4
+        out_shape += [sds((8, 3 * WIDE), F32)] + [sds((WIDE, D), BF)] * 4
+        scratch = [
             pltpu.VMEM((rows, 3 * WIDE), BF),
             pltpu.VMEM((rows, D), BF),
             pltpu.VMEM((rows, D), BF),
             pltpu.VMEM((rows, WIDE), BF),
-            pltpu.VMEM((WIDE, D), BF),
-        ],
+            pltpu.VMEM((4, WIDE, D), BF),
+            pltpu.SemaphoreType.DMA((4,)),
+            pltpu.SemaphoreType.DMA((4,)),
+        ]
+    return pl.pallas_call(
+        functools.partial(attn_backward, seq, group, base, count, last),
+        grid=(count + 4 if last else count,),
+        in_specs=in_specs,
+        out_specs=out_specs,
+        out_shape=out_shape,
+        input_output_aliases=aliases,
+        scratch_shapes=scratch,
         compiler_params=params(),
-    )(shard, log_total, qkv, first, attended, *more)
+    )(shard, log_total, qkv, first, attended, *more, *extra)
 
 
 def input_backward(seq, grad0, grad1, gh_ref, x_ref, vec_ref, qkv_w, out_ref, sum_ref):
@@ -664,7 +718,7 @@
     )(*grads, gh, x, vec, qkv_w)
 
 
-def pack(last_sum, back_sum, head0, head1, edge0, edge1, pre0, pre1, up0, up1, cot_sum, out_ref):
+def putter(out_ref):
     out_ref[...] = jnp.zeros_like(out_ref)
 
     def put(first, ref, row, col, width):
@@ -672,6 +726,11 @@
             at = col + LANES * k
             out_ref[first + k : first + k + 1, :] = ref[row : row + 1, at : at + LANES]
 
+    return put
+
+
+def pack(last_sum, back_sum, head0, head1, edge0, edge1, pre0, pre1, up0, up1, cot_sum, out_ref):
+    put = putter(out_ref)
     put(0, last_sum, 0, 0, D)
     put(6, last_sum, 1, 0, D)
     for group, (head, edge) in enumerate(((head0, edge0), (head1, edge1))):
@@ -801,28 +860,54 @@
         return out
 
 
+def pause_kernel(in_ref, out_ref):
+    out_ref[...] = in_ref[...]
+
+
+def pause(line, value):
+    return line(
+        pl.pallas_call(
+            pause_kernel,
+            out_shape=sds(value.shape, value.dtype),
+            cost_estimate=pl.CostEstimate(flops=10**11, bytes_accessed=10**8, transcendentals=0),
+        ),
+        value,
+    )
+
+
 class Sum:
-    def __init__(self, line, mine, other):
-        self.line, self.mine = line, mine
-        self.rows = mine.shape[1]
+    def __init__(self, line, across, same, mine_across, mine):
+        self.line, self.mine_across, self.mine = line, mine_across, mine
+        self.rows = mine.shape[0]
         rep = lax.axis_index("rep")
         self.near, self.far = rep % 2, rep // 2
         self.count = lax.axis_size("rep") // 2
-        self.came = swap(other, "shard", 1)
+        self.came_across, self.here = swap(across, "shard", 1), swap(same, "shard", 1)
 
     def side(self):
-        send = self.line(lambda m, c: (m.astype(F32) + c.astype(F32)).astype(BF), self.mine[1], self.came[1])
-        self.mine, self.here = self.mine[0], self.came[0]
+        add = lambda a, b: a.astype(F32) + b.astype(F32)
+        send = self.line(lambda a, b: add(a, b).astype(BF), self.mine_across, self.came_across)
         self.came = swap(send, "shard", 2)
+        self.mine = self.line(add, self.mine, self.here)
 
     def close(self):
-        def step(mine, here, came):
-            total = mine.astype(F32) + here.astype(F32) + came.astype(F32)
-            halves = total.reshape(2, self.rows // 2, D)
+        def step(mine, came):
+            halves = (mine + came.astype(F32)).reshape(2, self.rows // 2, D)
             return pick(halves, 1 - self.near).astype(BF), pick(halves, self.near)
 
-        send, self.half = self.line(step, self.mine, self.here, self.came)
+        send, self.half = self.line(step, self.mine, self.came)
         self.came = swap(send, "rep", 1)
+
+    def level(self, bit):
+        if bit == 2:
+            self.part = self.line(lambda a, b: (a + b.astype(F32)).astype(BF), self.half, self.came)
+        else:
+            self.part = self.line(lambda a, b: (a.astype(F32) + b.astype(F32)).astype(BF), self.part, self.came)
+        self.came = swap(self.part, "rep", bit)
+
+    def back_level(self):
+        self.half = self.line(lambda a, b: (a.astype(F32) + b.astype(F32)).astype(BF), self.part, self.came)
+        self.came = swap(self.half, "rep", 1)
 
     def along(self):
         def step(half, came):
@@ -841,6 +926,22 @@
 
         self.part = self.line(step, self.part, self.came)
         self.came = [turn(self.part, "rep", 2, d) for d in range(1, self.count)]
+
+    def gather(self):
+        def step(part, came):
+            for value in came:
+                part = part + value.astype(F32)
+            return part.astype(BF)
+
+        self.part = self.line(step, self.part, self.came)
+        self.came = lax.all_gather(self.part, "rep", axis=0, tiled=True)
+
+    def gathered(self):
+        def step(came):
+            parts = came.reshape(self.count, 2, self.rows // 2 // self.count, D)
+            return jnp.swapaxes(parts, 0, 1).reshape(self.rows, D)
+
+        return self.line(step, self.came)
 
     def back_close(self):
         def step(part, came):
@@ -864,10 +965,11 @@
     def __init__(self, line, value):
         self.line, self.value = line, value
         self.hops = [("shard", 1), ("shard", 2)]
-        bit = 1
+        bit = 2
         while bit < lax.axis_size("rep"):
             self.hops.append(("rep", bit))
             bit *= 2
+        self.hops.append(("rep", 1))
         self.came = swap(value, *self.hops.pop(0))
 
     def hop(self):
@@ -913,58 +1015,67 @@
     both0 = swap(across, "shard", 1)
     across1 = swap(send1, "shard", 2)
     boxes = (box0, near0, across0, both0)
-    result, gs, cot_sum, pre0, up0, other0, mine0 = line(
+    result, gs, cot_sum, pre0, up0, *grads = line(
         lambda *a: call_feed(seq, 0, *a), shard, extra, boxes, second, cot, hidden
     )
+    feed0 = Sum(line, *grads)
     both1 = swap(line(lambda a: a, across1), "shard", 1)
-    feed0 = Sum(line, mine0, other0)
     feed0.side()
     boxes = (box1, near1, across1, both1)
-    layer_output, gs, pre1, up1, other1, mine1 = line(
+    layer_output, gs, pre1, up1, *grads = line(
         lambda *a: call_feed(seq, 1, *a), shard, extra, boxes, second, cot, result, gs
     )
-    feed1 = Sum(line, mine1, other1)
+    feed1 = Sum(line, *grads)
     feed0.close()
     feed1.side()
-    grad0, head0, gh_low, ga, gh, back_sum, edge0, other2, mine2 = line(
-        lambda *a: call_attn_backward(seq, 0, *a), shard, log_total, qkv, first, attended, gs, hidden, cot, vec, proj_w
+    half = images // 2
+    common = (shard, log_total, qkv, first, attended)
+    more = (gs, hidden, cot, vec, proj_w)
+    before = line(lambda *a: call_attn_backward(seq, 0, 0, half, *a), *common, *more)
+    feed0.along()
+    grad0, head0, gh_low, ga, gh, back_sum, edge0, *grads = line(
+        lambda b, *a: call_attn_backward(seq, 0, half, images - half, *a, before=b), tuple(before), *common, *more
     )
-    attn0 = Sum(line, mine2, other2)
-    feed0.along()
+    attn0 = Sum(line, *grads)
+    feed0.gather()
     feed1.close()
     attn0.side()
-    grad1, head1, edge1, other3, mine3 = line(
-        lambda *a: call_attn_backward(seq, 1, *a), shard, log_total, qkv, first, attended, gh_low, ga
+    more = (gh_low, ga)
+    before = line(lambda *a: call_attn_backward(seq, 1, 0, half, *a), *common, *more)
+    feed1.along()
+    grad1, head1, edge1, *grads = line(
+        lambda b, *a: call_attn_backward(seq, 1, half, images - half, *a, before=b), tuple(before), *common, *more
     )
-    attn1 = Sum(line, mine3, other3)
-    feed0.back_along()
-    feed1.along()
+    attn1 = Sum(line, *grads)
+    feed1.back_along()
+    attn0.close()
+    head1 = pause(line, head1)
     attn1.side()
-    attn0.close()
     input_grad, last_sum = line(lambda *a: call_input_backward(seq, *a), (grad0, grad1), gh, x, vec, qkv_w)
     sums = line(call_pack, last_sum, back_sum, head0, head1, edge0, edge1, pre0, pre1, up0, up1, cot_sum)
+    bits = [2 << k for k in range((lax.axis_size("rep") // 2).bit_length() - 1)]
     sums = SumAll(line, sums)
-    feed0.back_close()
-    feed1.back_along()
-    attn0.along()
+    attn1.close()
+    attn0.level(2)
+    feed1.back_close()
     sums.hop()
-    attn1.close()
     sums.hop()
-    feed1.back_close()
-    attn0.back_along()
-    attn1.along()
+    for bit in bits[1:]:
+        attn0.level(bit)
+    attn1.level(2)
     sums.hop()
-    feed_box0 = feed0.end()
+    feed_box0 = feed0.gathered()
     while not sums.hop():
         pass
-    attn0.back_close()
-    attn1.back_along()
     feed_box1 = feed1.end()
-    attn_box0 = attn0.end()
-    attn1.back_close()
+    attn0.back_level()
+    for bit in bits[1:]:
+        attn1.level(bit)
     feed_grad, feed_change, feed_new = line(
         lambda *a: adam(FEED, *a, scale), shard, powers, sums.value, [feed_box0, feed_box1], feedforward_params, feedforward_moments
     )
+    attn1.back_level()
+    attn_box0 = attn0.end()
     attn_grad, attn_change, attn_new = line(
         lambda *a: adam(ATTN, *a, scale), shard, powers, sums.value, [attn_box0, attn1.end()], attention_params, attention_moments
     )

time: 420 us -> 378 us (0.900)
  waiting for transfers between devices: 96 us -> 60.9 us
  starting transfers between devices: 63.4 us -> 47.1 us
  local copies, waits for them, and re-layouts: 30.5 us -> 16.3 us
  between operations: 2.61 us -> 15.9 us
  Pallas kernels: 205 us -> 211 us
    ppermute x32 -> x39, waiting for transfers between devices: 88.6 us -> 53.1 us  [swap(): return lax.ppermute(value, axis, pairs)]
    ppermute x24 -> x9, starting transfers between devices: 34.7 us -> 13.3 us  [turn(): lax.ppermute(value, axis, [(i, (i + unit * distance) % size) for i in ran...]
    squeeze x8 -> x0, local copies, waits for them, and re-layouts: 10.4 us -> none  [side(): self.mine, self.here = (self.mine[0], self.came[0])]
    all_gather x0 -> x1, waiting for transfers between devices: none -> 7.82 us  [gather(): self.came = lax.all_gather(self.part, 'rep', axis=0, tiled=True)]
    pallas_call x2 -> x5, Pallas kernels: 53.6 us -> 61.1 us  [the longest x4 59.8 us: call_attn_backward(): pl.pallas_call(functools.partial(attn_backward, seq, group, base, count,...]
    ppermute x24 -> x9, waiting for transfers between devices: 7.38 us -> 0.02 us  [turn(): lax.ppermute(value, axis, [(i, (i + unit * distance) % size) for i in ran...]
    ppermute x32 -> x39, starting transfers between devices: 28.7 us -> 33.7 us  [swap(): return lax.ppermute(value, axis, pairs)]
    convert_element_type x4 -> x10, other arithmetic: 1.91 us -> 6.2 us  [the longest x4 5.8 us: side(): add(a, b).astype(BF)]
  transfers between devices with their start and end apart: 56 -> 49, of which waited for: 17 -> 14; matrix products, arithmetic and copies ran while one was open for 8% -> 8% of each run, Pallas kernels for 29% -> 54%
where the time goes in v1:
time: 378 us; the launch traced here: 371 us
  Pallas kernels  211 us (56%)
  waiting for transfers between devices  60.9 us (16%)
  starting transfers between devices  47.1 us (12%)
  other arithmetic  19.6 us (5%)
  local copies, waits for them, and re-layouts  16.3 us (4%)
  between operations  15.9 us (4%)
    pallas_call x2, Pallas kernels, call_feed(): pl.pallas_call(functools.partial(feed, seq, part, tall), grid=(ROW_STEPS...  73.2 us
    pallas_call x4, Pallas kernels, call_attn_backward(): pl.pallas_call(functools.partial(attn_backward, seq, group, base, count,...  59.8 us
    ppermute x39, waiting for transfers between devices, swap(): return lax.ppermute(value, axis, pairs)  53.1 us
    ppermute x39, starting transfers between devices, swap(): return lax.ppermute(value, axis, pairs)  33.7 us
    pallas_call x1, Pallas kernels, call_attn_forward(): pl.pallas_call(functools.partial(attn_forward, seq), grid=(images,), in_s...  29.6 us
    pallas_call x2, Pallas kernels, adam(): pl.pallas_call(functools.partial(adam_kernel, block, count, scale, len(bo...  23.8 us
    ppermute x9, starting transfers between devices, turn(): lax.ppermute(value, axis, [(i, (i + unit * distance) % size) for i in ran...  13.3 us
    pallas_call x1, Pallas kernels, call_input_backward(): pl.pallas_call(functools.partial(input_backward, seq), grid=(images // st...  13.2 us
  transfers between devices with their start and end apart: 49, of which 14 were waited for; matrix products, arithmetic and copies ran while one was open for 8% of the time, Pallas kernels for 54%

profile of v1, /device:TPU:0, one launch (start us, length us, event | category | flops | bytes accessed | tf_op | source)
XLA Modules:
  0.0 371.3 jit_solution(5365106892485872)
XLA Ops:
  7.2 3.0 shard_map.134
  10.2 3.0 collective-permute-start.2
  13.2 5.7 %shard_map.135 = (bf16[768,768]{1,0:T(8,128)(2,1)}, bf16[768,768]{1,0:T(8,128)(2,1)}, f32[72,128]{1,0:T(8,128)}) custom-call(s32[1]{0:T(128)} %bitcast.shard_ref, f32[1180992]{0:T(1024)} %refs_2_), custom_call_target="tpu_custom_call" | custom-call | tf_op jit(solution)/shard_map/pallas_call | solution.py:203
  19.7 1.6 collective-permute-start
  21.7 1.7 pad.7.clone
  25.2 1.6 pad.8.clone
  26.8 15.0 %collective-permute-done.1 = f32[144,128]{1,0:T(8,128)S(1)} collective-permute-done((f32[144,128]{1,0:T(8,128)S(1)}, f32[144,128]{1,0:T(8,128)S(1)}, u32[]{:S(2)}, u32[]{:S(2)}) %collective-permute-start.1) | collective-permute-done | bytes 73760 | tf_op jit(solution)/shard_map/ppermute | solution.py:837
  42.6 1.7 collective-permute-start.5
  45.5 1.0 copy-done.10
  46.5 29.6 %shard_map.136 = (bf16[1664,768]{1,0:T(8,128)(2,1)}, bf16[1664,2304]{1,0:T(8,128)(2,1)}, f32[8,12,208]{2,1,0:T(8,128)}, bf16[1664,768]{1,0:T(8,128)(2,1)}, f32[1...) custom-call(bf16[1664,768]{1,0:T(8,128)(2,1)} %bitcast.58, ...), custom_call_target="tpu_custom_call" | custom-call | tf_op jit(solution)/shard_map/pallas_call | solution.py:333
  76.5 1.4 collective-permute-start.8
  77.9 1.1 collective-permute-done.7.a3
  79.0 1.0 copy-done.14
  80.1 36.6 %shard_map.137 = (f32[1664,768]{1,0:T(8,128)}, f32[1664,768]{1,0:T(8,128)}, f32[8,768]{1,0:T(8,128)}, f32[8,1536]{1,0:T(8,128)}, f32[8,1536]{1,0:T(8,128)}, /*in...) custom-call(s32[1]{0:T(128)} %bitcast.shard_ref, ...), custom_call_target="tpu_custom_call" | custom-call | tf_op jit(solution)/shard_map/pallas_call | solution.py:472
  117.8 2.0 collective-permute-done.9
  119.8 1.7 add_convert_fusion.1
  121.5 1.6 collective-permute-start.13
  123.5 1.6 collective-permute-done.12.a3
  125.0 36.6 %shard_map.138 = (bf16[8,197,768]{2,1,0:T(8,128)(2,1)}, f32[1664,768]{1,0:T(8,128)}, f32[8,1536]{1,0:T(8,128)}, f32[8,1536]{1,0:T(8,128)}, bf16[768,768]{1,0:T(8...) custom-call(s32[1]{0:T(128)} %bitcast.shard_ref, ...), custom_call_target="tpu_custom_call" | custom-call | tf_op jit(solution)/shard_map/pallas_call | solution.py:472
  162.2 1.5 convert_add_fusion.2
  163.8 1.6 collective-permute-start.16
  165.4 2.7 add_convert_fusion
  168.1 1.4 collective-permute-start.20
  169.5 1.5 convert_add_fusion.1
  171.1 13.5 %shard_map.139 = (bf16[1664,1152]{1,0:T(8,128)(2,1)}, f32[8,384]{1,0:T(8,128)}, bf16[1664,768]{1,0:T(8,128)(2,1)}, bf16[1664,768]{1,0:T(8,128)(2,1)}, f32[1664,768]{1,0:T(8,128)}, /*index=5*/f32[8,768]{1,0:T(8,128)}) custom-call(s32[1]{0:T(128)} %bitcast.shard_ref, f32[8,12,208]{2,1,0:T(8,128)} %get-tuple-element.406.log_ref, ...), custom_call_target="tpu_custom_call" | custom-call | tf_op jit(solution)/shard_map/pallas_call | solution.py:672
  185.6 3.6 collective-permute-start.19
  189.2 1.0 collective-permute-start.17
  190.2 20.9 %shard_map.140 = (bf16[1664,1152]{1,0:T(8,128)(2,1)}, f32[8,384]{1,0:T(8,128)}, bf16[1664,768]{1,0:T(8,128)(2,1)}, bf16[1664,768]{1,0:T(8,128)(2,1)}, f32[1664,7...) custom-call(s32[1]{0:T(128)} %bitcast.shard_ref, ...), custom_call_target="tpu_custom_call", output_to_operand_aliasing={{2}: (14, {}), {0}: (15, {}), {3}: (16, {}), {4}: (17, {})} | custom-call | tf_op jit(solution)/shard_map/pallas_call | solution.py:672
  211.8 1.8 add_convert_fusion.11
  213.6 1.5 convert_add_fusion
  215.2 1.2 collective-permute-start.23
  216.4 1.3 add_convert_fusion.3
  218.5 9.2 %shard_map.141 = (bf16[1664,1152]{1,0:T(8,128)(2,1)}, f32[8,384]{1,0:T(8,128)}) custom-call(s32[1]{0:T(128)} %bitcast.shard_ref, f32[8,12,208]{2,1,0:T(8,128)} %get-tuple-element.406.log_ref, bf16[1664,2304]{1,0:T(8,128)(2,1)} %get-tuple-element.407.qkv_ref, bf16[1664,768]{1,0:T(8,128)(2,1)} %get-tuple-element.408.first_ref.refs_7_.refs_3_, ...), custom_call_target="tpu_custom_call" | custom-call | tf_op jit(solution)/shard_map/pallas_call | solution.py:672
  227.6 2.8 collective-permute-done.23
  230.6 2.9 collective-permute-start.26
  233.5 1.1 collective-permute-start.25
  234.6 16.2 %shard_map.142 = (bf16[1664,1152]{1,0:T(8,128)(2,1)}, f32[8,384]{1,0:T(8,128)}, f32[8,1152]{1,0:T(8,128)}, bf16[384,768]{1,0:T(8,128)(2,1)}, bf16[384,768]{1,0:T...) custom-call(s32[1]{0:T(128)} %bitcast.shard_ref, ...), custom_call_target="tpu_custom_call", output_to_operand_aliasing={{0}: (11, {})} | custom-call | tf_op jit(solution)/shard_map/pallas_call | solution.py:672
  251.8 1.4 shard_map.143.head1
  254.0 3.9 %collective-permute-start.34 = (bf16[96,768]{1,0:T(8,128)(2,1)S(1)}, bf16[96,768]{1,0:T(8,128)(2,1)S(1)}, u32[]{:S(2)}, u32[]{:S(2)}) collective-permute-start(bf16[96,768]{1,0:T(8,128)(2,1)S(1)} %add_convert_fusion.10), channel_id=1, source_target_pairs={{0,6},{1,7},{2,0},{3,1},{4,2},{5,3},{6,4},{7,5},{8,14},{9,15},{10,... | collective-permute-start | bytes 442376 | tf_op jit(solution)/shard_map/ppermute | solution.py:842
  258.8 1.1 collective-permute-start.31
  259.9 1.4 convert_add_fusion.5
  261.2 13.2 %shard_map.144 = (bf16[8,197,768]{2,1,0:T(8,128)(2,1)}, f32[8,768]{1,0:T(8,128)}) custom-call(bf16[1664,1152]{1,0:T(8,128)(2,1)} %get-tuple-element.434.grad0, bf16[1664,1152]{1,0:T(8,128)(2,1)} %get-tuple-element.435.grad1, f32[1664,768]{1,0:T(8,128)} %get-tuple-element.436.gh_ref, bf16[1664,768]{1,0:T(8,128)(2,1)} %bitcast.59, ...), custom_call_target="tpu_custom_call" | custom-call | tf_op jit(solution)/shard_map/pallas_call | solution.py:711
  274.5 1.7 shard_map.145
  276.5 2.8 collective-permute-start.37
  279.6 1.5 collective-permute-start.36
  281.1 1.0 collective-permute-start.38
  282.0 1.1 collective-permute-start.42
  284.1 1.0 collective-permute-start.39
  285.0 7.0 %collective-permute-done.37 = bf16[192,768]{1,0:T(8,128)(2,1)S(1)} collective-permute-done((bf16[192,768]{1,0:T(8,128)(2,1)S(1)}, bf16[192,768]{1,0:T(8,128)(2,1)S(1)}, u32[]{:S(2)}, u32[]{:S(2)}) %collective-permute-start.37) | collective-permute-done | bytes 294944 | tf_op jit(solution)/shard_map/ppermute | solution.py:837
  292.1 4.6 %collective-permute-done.38 = bf16[192,768]{1,0:T(8,128)(2,1)S(1)} collective-permute-done((bf16[192,768]{1,0:T(8,128)(2,1)S(1)}, bf16[192,768]{1,0:T(8,128)(2,1)S(1)}, u32[]{:S(2)}, u32[]{:S(2)}) %collective-permute-start.38) | collective-permute-done | bytes 294944 | tf_op jit(solution)/shard_map/ppermute | solution.py:837
  296.7 1.0 collective-permute-start.40
  297.7 7.8 %all-gather.2.cloned.1.call-done = bf16[768,768]{1,0:T(8,128)(2,1)} async-done(((bf16[96,768]{1,0:T(8,128)(2,1)}), bf16[768,768]{1,0:T(8,128)(2,1)}) %all-gather.2.cloned.1.call-update) | async-done | bytes 1179664 | tf_op jit(solution)/shard_map/all_gather | solution.py:937
  305.5 2.4 copy.26
  307.9 1.2 collective-permute-start.41
  309.4 1.5 collective-permute-start.44
  310.8 1.4 collective-permute-done.41
  313.0 1.1 pad_maximum_fusion.refs_1_
  314.1 9.9 %collective-permute-done.43 = bf16[192,768]{1,0:T(8,128)(2,1)S(1)} collective-permute-done((bf16[192,768]{1,0:T(8,128)(2,1)S(1)}, bf16[192,768]{1,0:T(8,128)(2,1)S(1)}, u32[]{:S(2)}, u32[]{:S(2)}) %collective-permute-start.43) | collective-permute-done | bytes 294944 | tf_op jit(solution)/shard_map/ppermute | solution.py:837
  325.5 1.6 collective-permute-start.46
  327.8 1.9 copy.27
  330.1 1.9 copy.28
  332.0 15.7 %shard_map.146 = (f32[1180992]{0:T(1024)}, f32[1180992]{0:T(1024)}, f32[2,1180992]{1,0:T(2,128)}) custom-call(s32[1]{0:T(128)} %bitcast.shard_ref, f32[2]{0:T(128)} %pad_maximum_fusion.3.power_ref, f32[144,128]{1,0:T(8,128)} %add.236.extra_ref, bf16[768,768]{1,0:T(8,128)(2,1)} %bitcast.64, bf16[768,768]{1,0:T(8,128)(2,1)} %pad_maximum_fusion.refs_1_, ...), custom_call_target="tpu_custom_call" | custom-call | tf_op jit(solution)/shard_map/pallas_call | solution.py:824
  349.2 5.7 %collective-permute-done.47 = bf16[192,768]{1,0:T(8,128)(2,1)S(1)} collective-permute-done((bf16[192,768]{1,0:T(8,128)(2,1)S(1)}, bf16[192,768]{1,0:T(8,128)(2,1)S(1)}, u32[]{:S(2)}, u32[]{:S(2)}) %collective-permute-start.47) | collective-permute-done | bytes 294944 | tf_op jit(solution)/shard_map/ppermute | solution.py:837
  355.8 8.2 %shard_map.147 = (f32[590784]{0:T(1024)}, f32[590784]{0:T(1024)}, f32[2,590784]{1,0:T(2,128)}) custom-call(s32[1]{0:T(128)} %bitcast.shard_ref, f32[2]{0:T(128)} %pad_maximum_fusion.3.power_ref, f32[144,128]{1,0:T(8,128)} %add.236.extra_ref, bf16[384,768]{1,0:T(8,128)(2,1)} %pad_maximum_fusion.1.refs_0_, bf16[384,768]{1,0:T(8,128)(2,1)} %pad_maximum_fusion.2.refs_1_, ...), custom_call_target="tpu_custom_call" | custom-call | tf_op jit(solution)/shard_map/pallas_call | solution.py:824
  (150 shorter events, 19.7 us)
Async XLA Ops:
  7.2 298.3 %all-gather.2.cloned.1.call-start = ((), (), s32[]{:S(2)}) async-start(), calls=%async_computation | async-start | bytes 1327104 | tf_op jit(solution)/shard_map/all_gather | solution.py:937
  10.2 32.2 %collective-permute-start.2 = (bf16[768,768]{1,0:T(8,128)(2,1)}, bf16[768,768]{1,0:T(8,128)(2,1)S(1)}, u32[]{:S(2)}, u32[]{:S(2)}) collective-permute-start(bf16[768,768]{1,0:T(8,128)(2,1)} %get-tuple-element.281.a0), channel_id=1, source_target_pairs={{0,16},{8,24},{16,0},{24,8},{1,17},{9,25},{17,1},{25,9},{2,18},{10... | collective-permute-start | bytes 3538952 | tf_op jit(solution)/shard_map/ppermute | solution.py:837
  13.2 5.7 %copy-start.19 = (f32[72,128]{1,0:T(8,128)S(1)}, f32[72,128]{1,0:T(8,128)}, u32[]{:S(2)}) copy-start(f32[72,128]{1,0:T(8,128)} %get-tuple-element.265) | copy-start | bytes 110596
  13.2 8.1 %copy-start.2 = (bf16[8,197,768]{2,0,1:T(8,128)(2,1)S(1)}, bf16[8,197,768]{2,0,1:T(8,128)(2,1)}, u32[]{:S(2)}) copy-start(bf16[8,197,768]{2,0,1:T(8,128)(2,1)} %param.7) | copy-start | bytes 7262212
  19.7 3.7 %collective-permute-start = (f32[144,128]{1,0:T(8,128)S(1)}, f32[144,128]{1,0:T(8,128)S(1)}, u32[]{:S(2)}, u32[]{:S(2)}) collective-permute-start(f32[144,128]{1,0:T(8,128)S(1)} %constant_dynamic-update-slice_fusion), channel_id=1, source_target_pairs={{0,8},{8,0},{16,24},{24,16},{1,9},{9,1},{17,25},{25,17},{2,10},{10... | collective-permute-start | bytes 221192 | tf_op jit(solution)/shard_map/ppermute | solution.py:837
  21.7 2.1 copy-start.6
  21.7 3.0 copy-start.3
  23.4 18.4 %collective-permute-start.1 = (f32[144,128]{1,0:T(8,128)S(1)}, f32[144,128]{1,0:T(8,128)S(1)}, u32[]{:S(2)}, u32[]{:S(2)}) collective-permute-start(f32[144,128]{1,0:T(8,128)S(1)} %add.192), channel_id=1, source_target_pairs={{0,16},{8,24},{16,0},{24,8},{1,17},{9,25},{17,1},{25,9},{2,18},{10... | collective-permute-start | bytes 221192 | tf_op jit(solution)/shard_map/ppermute | solution.py:837
  23.8 20.7 %collective-permute-start.3 = (bf16[768,768]{1,0:T(8,128)(2,1)S(1)}, bf16[768,768]{1,0:T(8,128)(2,1)S(1)}, u32[]{:S(2)}, u32[]{:S(2)}) collective-permute-start(bf16[768,768]{1,0:T(8,128)(2,1)S(1)} %copy-done.6), channel_id=1, source_target_pairs={{0,8},{8,0},{16,24},{24,16},{1,9},{9,1},{17,25},{25,17},{2,10},{10... | collective-permute-start | bytes 3538952 | tf_op jit(solution)/shard_map/ppermute | solution.py:837
  25.2 17.4 %copy-start.11 = (bf16[768,768]{1,0:T(8,128)(2,1)S(1)}, bf16[768,768]{1,0:T(8,128)(2,1)}, u32[]{:S(2)}) copy-start(bf16[768,768]{1,0:T(8,128)(2,1)} %get-tuple-element.295.a0) | copy-start | bytes 3538948
  42.4 2.9 copy-start.7
  42.4 2.8 collective-permute-start.4
  42.6 33.5 %collective-permute-start.5 = (bf16[768,768]{1,0:T(8,128)(2,1)S(1)}, bf16[768,768]{1,0:T(8,128)(2,1)S(1)}, u32[]{:S(2)}, u32[]{:S(2)}) collective-permute-start(bf16[768,768]{1,0:T(8,128)(2,1)S(1)} %copy-done.11), channel_id=1, source_target_pairs={{0,16},{8,24},{16,0},{24,8},{1,17},{9,25},{17,1},{25,9},{2,18},{10... | collective-permute-start | bytes 3538952 | tf_op jit(solution)/shard_map/ppermute | solution.py:837
  44.3 33.6 %collective-permute-start.6 = (bf16[768,768]{1,0:T(8,128)(2,1)S(1)}, bf16[768,768]{1,0:T(8,128)(2,1)S(1)}, u32[]{:S(2)}, u32[]{:S(2)}) collective-permute-start(bf16[768,768]{1,0:T(8,128)(2,1)S(1)} %copy-done.11), channel_id=1, source_target_pairs={{0,8},{8,0},{16,24},{24,16},{1,9},{9,1},{17,25},{25,17},{2,10},{10... | collective-permute-start | bytes 3538952 | tf_op jit(solution)/shard_map/ppermute | solution.py:837
  76.1 4.0 %copy-start.12 = (bf16[768,768]{1,0:T(8,128)(2,1)}, bf16[768,768]{1,0:T(8,128)(2,1)S(1)}, u32[]{:S(2)}) copy-start(bf16[768,768]{1,0:T(8,128)(2,1)S(1)} %collective-permute-done.5.a2) | copy-start | bytes 3538948
  76.1 2.9 collective-permute-start.7
  76.5 41.1 %collective-permute-start.8 = (bf16[768,768]{1,0:T(8,128)(2,1)}, bf16[768,768]{1,0:T(8,128)(2,1)}, u32[]{:S(2)}, u32[]{:S(2)}) collective-permute-start(bf16[768,768]{1,0:T(8,128)(2,1)} %get-tuple-element.317.a0), channel_id=1, source_target_pairs={{0,16},{8,24},{16,0},{24,8},{1,17},{9,25},{17,1},{25,9},{2,18},{10... | collective-permute-start | bytes 3538952 | tf_op jit(solution)/shard_map/ppermute | solution.py:837
  77.9 2.2 copy-start.13
  116.7 3.1 collective-permute-start.9
  117.1 6.1 %collective-permute-start.10 = (bf16[768,768]{1,0:T(8,128)(2,1)}, bf16[768,768]{1,0:T(8,128)(2,1)S(1)}, u32[]{:S(2)}, u32[]{:S(2)}) collective-permute-start(bf16[768,768]{1,0:T(8,128)(2,1)} %get-tuple-element.310), channel_id=1, source_target_pairs={{0,8},{8,0},{16,24},{24,16},{1,9},{9,1},{17,25},{25,17},{2,10},{10... | collective-permute-start | bytes 3538952 | tf_op jit(solution)/shard_map/ppermute | solution.py:837
  117.3 6.2 %collective-permute-start.11 = (bf16[768,768]{1,0:T(8,128)(2,1)}, bf16[768,768]{1,0:T(8,128)(2,1)}, u32[]{:S(2)}, u32[]{:S(2)}) collective-permute-start(bf16[768,768]{1,0:T(8,128)(2,1)} %get-tuple-element.317.a0), channel_id=1, source_target_pairs={{0,8},{8,0},{16,24},{24,16},{1,9},{9,1},{17,25},{25,17},{2,10},{10... | collective-permute-start | bytes 3538952 | tf_op jit(solution)/shard_map/ppermute | solution.py:837
  117.6 7.4 %collective-permute-start.12 = (bf16[768,768]{1,0:T(8,128)(2,1)}, bf16[768,768]{1,0:T(8,128)(2,1)}, u32[]{:S(2)}, u32[]{:S(2)}) collective-permute-start(bf16[768,768]{1,0:T(8,128)(2,1)} %collective-permute-done.8.a2), channel_id=1, source_target_pairs={{0,8},{8,0},{16,24},{24,16},{1,9},{9,1},{17,25},{25,17},{2,10},{10... | collective-permute-start | bytes 3538952 | tf_op jit(solution)/shard_map/ppermute | solution.py:837
  119.8 3.4 copy-start.8
  121.5 40.7 %collective-permute-start.13 = (bf16[768,768]{1,0:T(8,128)(2,1)S(1)}, bf16[768,768]{1,0:T(8,128)(2,1)}, u32[]{:S(2)}, u32[]{:S(2)}) collective-permute-start(bf16[768,768]{1,0:T(8,128)(2,1)S(1)} %add_convert_fusion.1), channel_id=1, source_target_pairs={{0,16},{8,24},{16,0},{24,8},{1,17},{9,25},{17,1},{25,9},{2,18},{10... | collective-permute-start | bytes 3538952 | tf_op jit(solution)/shard_map/ppermute | solution.py:837
  161.6 3.8 %collective-permute-start.14 = (bf16[768,768]{1,0:T(8,128)(2,1)}, bf16[768,768]{1,0:T(8,128)(2,1)}, u32[]{:S(2)}, u32[]{:S(2)}) collective-permute-start(bf16[768,768]{1,0:T(8,128)(2,1)} %get-tuple-element.330), channel_id=1, source_target_pairs={{0,8},{8,0},{16,24},{24,16},{1,9},{9,1},{17,25},{25,17},{2,10},{10... | collective-permute-start | bytes 3538952 | tf_op jit(solution)/shard_map/ppermute | solution.py:837
  162.0 7.5 %collective-permute-start.15 = (bf16[768,768]{1,0:T(8,128)(2,1)}, bf16[768,768]{1,0:T(8,128)(2,1)}, u32[]{:S(2)}, u32[]{:S(2)}) collective-permute-start(bf16[768,768]{1,0:T(8,128)(2,1)} %get-tuple-element.334), channel_id=1, source_target_pairs={{0,8},{8,0},{16,24},{24,16},{1,9},{9,1},{17,25},{25,17},{2,10},{10... | collective-permute-start | bytes 3538952 | tf_op jit(solution)/shard_map/ppermute | solution.py:837
  163.7 1.7 copy-start.4
  163.8 20.9 %collective-permute-start.16 = (bf16[384,768]{1,0:T(8,128)(2,1)S(1)}, bf16[384,768]{1,0:T(8,128)(2,1)S(1)}, u32[]{:S(2)}, u32[]{:S(2)}) collective-permute-start(bf16[384,768]{1,0:T(8,128)(2,1)S(1)} %fusion), channel_id=1, source_target_pairs={{0,1},{1,0},{2,3},{3,2},{4,5},{5,4},{6,7},{7,6},{8,9},{9,8},{10,11... | collective-permute-start | bytes 1769480 | tf_op jit(solution)/shard_map/ppermute | solution.py:837
  165.4 4.1 %copy-start.5 = (bf16[768,768]{1,0:T(8,128)(2,1)S(1)}, bf16[768,768]{1,0:T(8,128)(2,1)}, u32[]{:S(2)}) copy-start(bf16[768,768]{1,0:T(8,128)(2,1)} %get-tuple-element.335) | copy-start | bytes 3538948
  168.1 45.4 %collective-permute-start.20 = (bf16[768,768]{1,0:T(8,128)(2,1)}, bf16[768,768]{1,0:T(8,128)(2,1)}, u32[]{:S(2)}, u32[]{:S(2)}) collective-permute-start(bf16[768,768]{1,0:T(8,128)(2,1)} %add_convert_fusion), channel_id=1, source_target_pairs={{0,16},{8,24},{16,0},{24,8},{1,17},{9,25},{17,1},{25,9},{2,18},{10... | collective-permute-start | bytes 3538952 | tf_op jit(solution)/shard_map/ppermute | solution.py:837
  185.6 25.6 %collective-permute-start.19 = (bf16[96,768]{1,0:T(8,128)(2,1)}, bf16[96,768]{1,0:T(8,128)(2,1)}, u32[]{:S(2)}, u32[]{:S(2)}) collective-permute-start(bf16[96,768]{1,0:T(8,128)(2,1)} %get-tuple-element.535), channel_id=1, source_target_pairs={{0,6},{1,7},{2,0},{3,1},{4,2},{5,3},{6,4},{7,5},{8,14},{9,15},{10,... | collective-permute-start | bytes 442376 | tf_op jit(solution)/shard_map/ppermute | solution.py:842
  189.2 22.6 %collective-permute-start.18 = (bf16[96,768]{1,0:T(8,128)(2,1)}, bf16[96,768]{1,0:T(8,128)(2,1)}, u32[]{:S(2)}, u32[]{:S(2)}) collective-permute-start(bf16[96,768]{1,0:T(8,128)(2,1)} %get-tuple-element.536), channel_id=1, source_target_pairs={{0,4},{1,5},{2,6},{3,7},{4,0},{5,1},{6,2},{7,3},{8,12},{9,13},{10,... | collective-permute-start | bytes 442376 | tf_op jit(solution)/shard_map/ppermute | solution.py:842
  189.2 22.6 %collective-permute-start.17 = (bf16[96,768]{1,0:T(8,128)(2,1)}, bf16[96,768]{1,0:T(8,128)(2,1)}, u32[]{:S(2)}, u32[]{:S(2)}) collective-permute-start(bf16[96,768]{1,0:T(8,128)(2,1)} %get-tuple-element.537), channel_id=1, source_target_pairs={{0,2},{1,3},{2,4},{3,5},{4,6},{5,7},{6,0},{7,1},{8,10},{9,11},{10,... | collective-permute-start | bytes 442376 | tf_op jit(solution)/shard_map/ppermute | solution.py:842
  211.1 5.3 %collective-permute-start.21 = (bf16[384,768]{1,0:T(8,128)(2,1)}, bf16[384,768]{1,0:T(8,128)(2,1)}, u32[]{:S(2)}, u32[]{:S(2)}) collective-permute-start(bf16[384,768]{1,0:T(8,128)(2,1)} %get-tuple-element.385), channel_id=1, source_target_pairs={{0,8},{8,0},{16,24},{24,16},{1,9},{9,1},{17,25},{25,17},{2,10},{10... | collective-permute-start | bytes 1769480 | tf_op jit(solution)/shard_map/ppermute | solution.py:837
  211.2 7.2 %collective-permute-start.22 = (bf16[384,768]{1,0:T(8,128)(2,1)}, bf16[384,768]{1,0:T(8,128)(2,1)S(1)}, u32[]{:S(2)}, u32[]{:S(2)}) collective-permute-start(bf16[384,768]{1,0:T(8,128)(2,1)} %get-tuple-element.389), channel_id=1, source_target_pairs={{0,8},{8,0},{16,24},{24,16},{1,9},{9,1},{17,25},{25,17},{2,10},{10... | collective-permute-start | bytes 1769480 | tf_op jit(solution)/shard_map/ppermute | solution.py:837
  215.2 15.3 %collective-permute-start.23 = (bf16[384,768]{1,0:T(8,128)(2,1)S(1)}, bf16[384,768]{1,0:T(8,128)(2,1)S(1)}, u32[]{:S(2)}, u32[]{:S(2)}) collective-permute-start(bf16[384,768]{1,0:T(8,128)(2,1)S(1)} %fusion.1), channel_id=1, source_target_pairs={{0,1},{1,0},{2,3},{3,2},{4,5},{5,4},{6,7},{7,6},{8,9},{9,8},{10,11... | collective-permute-start | bytes 1769480 | tf_op jit(solution)/shard_map/ppermute | solution.py:837
  216.4 2.0 copy-start.17
  217.7 33.9 %collective-permute-start.27 = (bf16[384,768]{1,0:T(8,128)(2,1)S(1)}, bf16[384,768]{1,0:T(8,128)(2,1)S(1)}, u32[]{:S(2)}, u32[]{:S(2)}) collective-permute-start(bf16[384,768]{1,0:T(8,128)(2,1)S(1)} %add_convert_fusion.3), channel_id=1, source_target_pairs={{0,16},{8,24},{16,0},{24,8},{1,17},{9,25},{17,1},{25,9},{2,18},{10... | collective-permute-start | bytes 1769480 | tf_op jit(solution)/shard_map/ppermute | solution.py:837
  230.6 20.3 %collective-permute-start.26 = (bf16[96,768]{1,0:T(8,128)(2,1)S(1)}, bf16[96,768]{1,0:T(8,128)(2,1)S(1)}, u32[]{:S(2)}, u32[]{:S(2)}) collective-permute-start(bf16[96,768]{1,0:T(8,128)(2,1)S(1)} %get-tuple-element.532), channel_id=1, source_target_pairs={{0,6},{1,7},{2,0},{3,1},{4,2},{5,3},{6,4},{7,5},{8,14},{9,15},{10,... | collective-permute-start | bytes 442376 | tf_op jit(solution)/shard_map/ppermute | solution.py:842
  233.5 18.0 %collective-permute-start.25 = (bf16[96,768]{1,0:T(8,128)(2,1)S(1)}, bf16[96,768]{1,0:T(8,128)(2,1)S(1)}, u32[]{:S(2)}, u32[]{:S(2)}) collective-permute-start(bf16[96,768]{1,0:T(8,128)(2,1)S(1)} %get-tuple-element.533), channel_id=1, source_target_pairs={{0,4},{1,5},{2,6},{3,7},{4,0},{5,1},{6,2},{7,3},{8,12},{9,13},{10,... | collective-permute-start | bytes 442376 | tf_op jit(solution)/shard_map/ppermute | solution.py:842
  234.6 16.9 %collective-permute-start.24 = (bf16[96,768]{1,0:T(8,128)(2,1)S(1)}, bf16[96,768]{1,0:T(8,128)(2,1)S(1)}, u32[]{:S(2)}, u32[]{:S(2)}) collective-permute-start(bf16[96,768]{1,0:T(8,128)(2,1)S(1)} %get-tuple-element.534), channel_id=1, source_target_pairs={{0,2},{1,3},{2,4},{3,5},{4,6},{5,7},{6,0},{7,1},{8,10},{9,11},{10,... | collective-permute-start | bytes 442376 | tf_op jit(solution)/shard_map/ppermute | solution.py:842
  250.9 2.3 collective-permute-start.28
  251.0 7.8 %collective-permute-start.29 = (bf16[384,768]{1,0:T(8,128)(2,1)}, bf16[384,768]{1,0:T(8,128)(2,1)}, u32[]{:S(2)}, u32[]{:S(2)}) collective-permute-start(bf16[384,768]{1,0:T(8,128)(2,1)} %get-tuple-element.427), channel_id=1, source_target_pairs={{0,8},{8,0},{16,24},{24,16},{1,9},{9,1},{17,25},{25,17},{2,10},{10... | collective-permute-start | bytes 1769480 | tf_op jit(solution)/shard_map/ppermute | solution.py:837
  253.3 22.8 %collective-permute-start.30 = (bf16[384,768]{1,0:T(8,128)(2,1)S(1)}, bf16[384,768]{1,0:T(8,128)(2,1)S(1)}, u32[]{:S(2)}, u32[]{:S(2)}) collective-permute-start(bf16[384,768]{1,0:T(8,128)(2,1)S(1)} %add_convert_fusion.2), channel_id=1, source_target_pairs={{0,16},{8,24},{16,0},{24,8},{1,17},{9,25},{17,1},{25,9},{2,18},{10... | collective-permute-start | bytes 1769480 | tf_op jit(solution)/shard_map/ppermute | solution.py:837
  254.0 25.4 %collective-permute-start.34 = (bf16[96,768]{1,0:T(8,128)(2,1)S(1)}, bf16[96,768]{1,0:T(8,128)(2,1)S(1)}, u32[]{:S(2)}, u32[]{:S(2)}) collective-permute-start(bf16[96,768]{1,0:T(8,128)(2,1)S(1)} %add_convert_fusion.10), channel_id=1, source_target_pairs={{0,6},{1,7},{2,0},{3,1},{4,2},{5,3},{6,4},{7,5},{8,14},{9,15},{10,... | collective-permute-start | bytes 442376 | tf_op jit(solution)/shard_map/ppermute | solution.py:842
  257.9 21.5 %collective-permute-start.33 = (bf16[96,768]{1,0:T(8,128)(2,1)S(1)}, bf16[96,768]{1,0:T(8,128)(2,1)S(1)}, u32[]{:S(2)}, u32[]{:S(2)}) collective-permute-start(bf16[96,768]{1,0:T(8,128)(2,1)S(1)} %add_convert_fusion.10), channel_id=1, source_target_pairs={{0,4},{1,5},{2,6},{3,7},{4,0},{5,1},{6,2},{7,3},{8,12},{9,13},{10,... | collective-permute-start | bytes 442376 | tf_op jit(solution)/shard_map/ppermute | solution.py:842
  257.9 21.5 %collective-permute-start.32 = (bf16[96,768]{1,0:T(8,128)(2,1)S(1)}, bf16[96,768]{1,0:T(8,128)(2,1)S(1)}, u32[]{:S(2)}, u32[]{:S(2)}) collective-permute-start(bf16[96,768]{1,0:T(8,128)(2,1)S(1)} %add_convert_fusion.10), channel_id=1, source_target_pairs={{0,2},{1,3},{2,4},{3,5},{4,6},{5,7},{6,0},{7,1},{8,10},{9,11},{10,... | collective-permute-start | bytes 442376 | tf_op jit(solution)/shard_map/ppermute | solution.py:842
  258.8 17.7 %collective-permute-start.31 = (bf16[192,768]{1,0:T(8,128)(2,1)S(1)}, bf16[192,768]{1,0:T(8,128)(2,1)S(1)}, u32[]{:S(2)}, u32[]{:S(2)}) collective-permute-start(bf16[192,768]{1,0:T(8,128)(2,1)S(1)} %fusion.2), channel_id=1, source_target_pairs={{0,1},{1,0},{2,3},{3,2},{4,5},{5,4},{6,7},{7,6},{8,9},{9,8},{10,11... | collective-permute-start | bytes 884744 | tf_op jit(solution)/shard_map/ppermute | solution.py:837
  276.1 3.4 collective-permute-start.35
  276.5 3.0 copy-start.18
  276.5 15.4 %collective-permute-start.37 = (bf16[192,768]{1,0:T(8,128)(2,1)S(1)}, bf16[192,768]{1,0:T(8,128)(2,1)S(1)}, u32[]{:S(2)}, u32[]{:S(2)}) collective-permute-start(bf16[192,768]{1,0:T(8,128)(2,1)S(1)} %add_convert_fusion.9), channel_id=1, source_target_pairs={{0,2},{1,3},{2,0},{3,1},{4,6},{5,7},{6,4},{7,5},{8,10},{9,11},{10,... | collective-permute-start | bytes 884744 | tf_op jit(solution)/shard_map/ppermute | solution.py:837
  279.6 4.5 %collective-permute-start.36 = (f32[144,128]{1,0:T(8,128)S(1)}, f32[144,128]{1,0:T(8,128)S(1)}, u32[]{:S(2)}, u32[]{:S(2)}) collective-permute-start(f32[144,128]{1,0:T(8,128)S(1)} %add.230), channel_id=1, source_target_pairs={{0,16},{8,24},{16,0},{24,8},{1,17},{9,25},{17,1},{25,9},{2,18},{10... | collective-permute-start | bytes 221192 | tf_op jit(solution)/shard_map/ppermute | solution.py:837
  281.1 15.5 %collective-permute-start.38 = (bf16[192,768]{1,0:T(8,128)(2,1)S(1)}, bf16[192,768]{1,0:T(8,128)(2,1)S(1)}, u32[]{:S(2)}, u32[]{:S(2)}) collective-permute-start(bf16[192,768]{1,0:T(8,128)(2,1)S(1)} %fusion.3), channel_id=1, source_target_pairs={{0,1},{1,0},{2,3},{3,2},{4,5},{5,4},{6,7},{7,6},{8,9},{9,8},{10,11... | collective-permute-start | bytes 884744 | tf_op jit(solution)/shard_map/ppermute | solution.py:837
  282.0 30.9 %collective-permute-start.42 = (bf16[384,768]{1,0:T(8,128)(2,1)S(1)}, bf16[384,768]{1,0:T(8,128)(2,1)S(1)}, u32[]{:S(2)}, u32[]{:S(2)}) collective-permute-start(bf16[384,768]{1,0:T(8,128)(2,1)S(1)} %bitcast.73), channel_id=1, source_target_pairs={{0,1},{1,0},{2,3},{3,2},{4,5},{5,4},{6,7},{7,6},{8,9},{9,8},{10,11... | collective-permute-start | bytes 1769480 | tf_op jit(solution)/shard_map/ppermute | solution.py:837
  284.1 12.6 %collective-permute-start.39 = (f32[144,128]{1,0:T(8,128)S(1)}, f32[144,128]{1,0:T(8,128)S(1)}, u32[]{:S(2)}, u32[]{:S(2)}) collective-permute-start(f32[144,128]{1,0:T(8,128)S(1)} %add.231), channel_id=1, source_target_pairs={{0,2},{1,3},{2,0},{3,1},{4,6},{5,7},{6,4},{7,5},{8,10},{9,11},{10,... | collective-permute-start | bytes 221192 | tf_op jit(solution)/shard_map/ppermute | solution.py:837
  296.7 11.2 %collective-permute-start.40 = (f32[144,128]{1,0:T(8,128)S(1)}, f32[144,128]{1,0:T(8,128)S(1)}, u32[]{:S(2)}, u32[]{:S(2)}) collective-permute-start(f32[144,128]{1,0:T(8,128)S(1)} %add.234), channel_id=1, source_target_pairs={{0,4},{1,5},{2,6},{3,7},{4,0},{5,1},{6,2},{7,3},{8,12},{9,13},{10,... | collective-permute-start | bytes 221192 | tf_op jit(solution)/shard_map/ppermute | solution.py:837
  307.9 4.4 %collective-permute-start.41 = (f32[144,128]{1,0:T(8,128)S(1)}, f32[144,128]{1,0:T(8,128)S(1)}, u32[]{:S(2)}, u32[]{:S(2)}) collective-permute-start(f32[144,128]{1,0:T(8,128)S(1)} %add.235), channel_id=1, source_target_pairs={{0,1},{1,0},{2,3},{3,2},{4,5},{5,4},{6,7},{7,6},{8,9},{9,8},{10,11... | collective-permute-start | bytes 221192 | tf_op jit(solution)/shard_map/ppermute | solution.py:837
  309.1 14.9 %collective-permute-start.43 = (bf16[192,768]{1,0:T(8,128)(2,1)S(1)}, bf16[192,768]{1,0:T(8,128)(2,1)S(1)}, u32[]{:S(2)}, u32[]{:S(2)}) collective-permute-start(bf16[192,768]{1,0:T(8,128)(2,1)S(1)} %add_convert_fusion.8), channel_id=1, source_target_pairs={{0,4},{1,5},{2,6},{3,7},{4,0},{5,1},{6,2},{7,3},{8,12},{9,13},{10,... | collective-permute-start | bytes 884744 | tf_op jit(solution)/shard_map/ppermute | solution.py:837
  309.4 14.7 %collective-permute-start.44 = (bf16[192,768]{1,0:T(8,128)(2,1)S(1)}, bf16[192,768]{1,0:T(8,128)(2,1)S(1)}, u32[]{:S(2)}, u32[]{:S(2)}) collective-permute-start(bf16[192,768]{1,0:T(8,128)(2,1)S(1)} %add_convert_fusion.7), channel_id=1, source_target_pairs={{0,2},{1,3},{2,0},{3,1},{4,6},{5,7},{6,4},{7,5},{8,10},{9,11},{10,... | collective-permute-start | bytes 884744 | tf_op jit(solution)/shard_map/ppermute | solution.py:837
  313.0 14.8 %copy-start = (bf16[8,197,768]{2,1,0:T(8,128)(2,1)S(1)}, bf16[8,197,768]{2,1,0:T(8,128)(2,1)}, u32[]{:S(2)}) copy-start(bf16[8,197,768]{2,1,0:T(8,128)(2,1)} %get-tuple-element.522) | copy-start | bytes 7262212
  324.1 23.5 %collective-permute-start.45 = (bf16[192,768]{1,0:T(8,128)(2,1)S(1)}, bf16[192,768]{1,0:T(8,128)(2,1)S(1)}, u32[]{:S(2)}, u32[]{:S(2)}) collective-permute-start(bf16[192,768]{1,0:T(8,128)(2,1)S(1)} %add_convert_fusion.5), channel_id=1, source_target_pairs={{0,4},{1,5},{2,6},{3,7},{4,0},{5,1},{6,2},{7,3},{8,12},{9,13},{10,... | collective-permute-start | bytes 884744 | tf_op jit(solution)/shard_map/ppermute | solution.py:837
  325.5 22.7 %collective-permute-start.46 = (bf16[192,768]{1,0:T(8,128)(2,1)S(1)}, bf16[192,768]{1,0:T(8,128)(2,1)S(1)}, u32[]{:S(2)}, u32[]{:S(2)}) collective-permute-start(bf16[192,768]{1,0:T(8,128)(2,1)S(1)} %add_convert_fusion.6), channel_id=1, source_target_pairs={{0,1},{1,0},{2,3},{3,2},{4,5},{5,4},{6,7},{7,6},{8,9},{9,8},{10,11... | collective-permute-start | bytes 884744 | tf_op jit(solution)/shard_map/ppermute | solution.py:837
  327.8 2.4 copy-start.1
  347.7 7.2 %collective-permute-start.47 = (bf16[192,768]{1,0:T(8,128)(2,1)S(1)}, bf16[192,768]{1,0:T(8,128)(2,1)S(1)}, u32[]{:S(2)}, u32[]{:S(2)}) collective-permute-start(bf16[192,768]{1,0:T(8,128)(2,1)S(1)} %add_convert_fusion.4), channel_id=1, source_target_pairs={{0,1},{1,0},{2,3},{3,2},{4,5},{5,4},{6,7},{7,6},{8,9},{9,8},{10,11... | collective-permute-start | bytes 884744 | tf_op jit(solution)/shard_map/ppermute | solution.py:837
  (5 other events, 5.7 us)
Sparse Core Ops, SparseCore 0:
  254.1 51.3 all-gather.1
